TPU v7x, 256 devices: a whole 4x4x8 slice. The times are simulated.
256 devices in a mesh: dp: 4 (over y_hi, core), ctx: 64 (over y_lo, x, z).
Axes of the slice: x: 4, y: 4 (y_hi: 2, y_lo: 2; y = y_hi * 2 + y_lo), z: 8, core: 2. Of those that a mesh axis runs over, the one named last changes fastest.
Arguments:
- queries: bfloat16 [65536, 1024], P(('dp', 'ctx')), parts along dimension 0, may hold values from -128 to 128
- keys: bfloat16 [65536, 128], P(('dp', 'ctx')), parts along dimension 0, may hold values from -4.1 to 4.1
- values: bfloat16 [65536, 128], P(('dp', 'ctx')), parts along dimension 0, may hold values from -6 to 6
- positions: int32 [65536], P(('dp', 'ctx')), parts along dimension 0, may hold values from 0 to 16383, as said below
- valid_length: int32 [4], P('dp'), parts along dimension 0, may hold values from 8192 to 16384
Outputs:
- attended: bfloat16 [65536, 1024], P(('dp', 'ctx')), parts along dimension 0
- log_sum_exp: float32 [8, 65536], P(None, ('dp', 'ctx')), parts along dimension 1
There are 4 independent parts, one for each index of `dp`. A program takes and returns all parts, laid end to end along the dimension named above; each array names one. Nothing has to cross between parts.
Inputs may be any that keep to these rules, and one draw needn't show every extreme that they name: One sequence's positions are a permutation of its token indices made of aligned runs of 128 consecutive values; each device holds whole runs, in pairs whose first positions sum to 16256.
All inputs are finite; a program needn't handle non-finite values.
Results may differ from a plain program's by a relative error of at most 0.0075.
Values may be sent and summed in bfloat16 or wider, within the bound.
No kernel may reach another device: no remote copies, remote signals or barrier semaphores. Data moves between devices by JAX's collectives and lax.ppermute only.
A program may use at most 64 MiB of HBM per device.

v0:
```python
import math

import jax
import jax.numpy as jnp
from jax import lax
from jax.sharding import PartitionSpec as P

SPAN = 128


negative_floor = -1e30


def shards(queries, keys, values, positions, valid_length):
    tok_rows = queries.shape[0]
    depth = keys.shape[1]
    heads = queries.shape[1] // depth
    query3 = queries.reshape(tok_rows, heads, depth)
    length = valid_length[0]
    latest = jnp.max(positions)
    scale = 1.0 / math.sqrt(depth)

    def update(state, key_block, value_block, pos_block):
        row_max, total, accum = state
        scores = (
            jnp.einsum("thd,kd->htk", query3, key_block, preferred_element_type=jnp.float32) * scale
        )
        visible = (pos_block[None, :] <= positions[:, None]) & (pos_block < length)[None, :]
        scores = jnp.where(visible[None], scores, negative_floor)
        new_max = jnp.maximum(row_max, jnp.max(scores, axis=-1))
        expo = jnp.where(visible[None], jnp.exp(scores - new_max[..., None]), 0.0)
        factor = jnp.exp(row_max - new_max)
        total = total * factor + jnp.sum(expo, axis=-1)
        weights = expo.astype(jnp.bfloat16)
        accum = accum * jnp.transpose(factor)[:, :, None] + jnp.einsum(
            "htk,kd->thd", weights, value_block, preferred_element_type=jnp.float32
        )
        return (new_max, total, accum)

    initial = (
        jnp.full((heads, tok_rows), negative_floor, jnp.float32),
        jnp.zeros((heads, tok_rows), jnp.float32),
        jnp.zeros((tok_rows, heads, depth), jnp.float32),
    )
    key_rows = lax.all_gather(keys, "ctx", axis=0, tiled=True)
    value_rows = lax.all_gather(values, "ctx", axis=0, tiled=True)
    key_pos = lax.all_gather(positions, "ctx", axis=0, tiled=True)
    count = key_rows.shape[0] // SPAN

    def visit(index, inner):
        first = index * SPAN
        key_block = lax.dynamic_slice_in_dim(key_rows, first, SPAN, 0)
        value_block = lax.dynamic_slice_in_dim(value_rows, first, SPAN, 0)
        pos_block = lax.dynamic_slice_in_dim(key_pos, first, SPAN, 0)
        lowest = jnp.min(pos_block)
        needed = (lowest <= latest) & (lowest < length)
        return lax.cond(
            needed,
            lambda held: update(held, key_block, value_block, pos_block),
            lambda held: held,
            inner,
        )

    state = lax.fori_loop(0, count, visit, initial)
    row_max, total, accum = state
    mixed = accum / jnp.transpose(total)[:, :, None]
    attended = mixed.astype(jnp.bfloat16).reshape(tok_rows, heads * depth)
    log_sum_exp = row_max + jnp.log(total)
    return (attended, log_sum_exp)


def solution(mesh):
    placed = (
        P(("dp", "ctx"), None),
        P(("dp", "ctx"), None),
        P(("dp", "ctx"), None),
        P(("dp", "ctx")),
        P("dp"),
    )
    return jax.shard_map(
        shards,
        mesh=mesh,
        in_specs=placed,
        out_specs=(P(("dp", "ctx"), None), P(None, ("dp", "ctx"))),
        check_vma=False,
    )
```

profile of v0, /device:TPU:40, one launch (start us, length us, event | category | flops | bytes accessed | tf_op | source)
XLA Modules:
  0.0 1563.5 jit_solution(3979258971618973544)
XLA Ops:
  11.5 153.0 %all-gather = s32[64,1,256]{2,1,0:T(1,128)S(1)} all-gather(s32[1,1,256]{2,1,0:T(1,128)} %bitcast.32), channel_id=1, replica_groups=mesh['dp'=4,'ctx'=64] {'ctx'}, dimensions={0}, use_global_device_ids=true | all-gather | bytes 66560 | tf_op jit(solution)/shard_map/all_gather | solution.py:47
  164.5 150.1 %all-gather.4.cloned.1.call-done = bf16[16384,128]{1,0:T(8,128)(2,1)} async-done(((bf16[256,128]{1,0:T(8,128)(2,1)}), bf16[16384,128]{1,0:T(8,128)(2,1)}) %all-gather.4.cloned.1.call-update) | async-done | bytes 4194320 | tf_op jit(solution)/shard_map/all_gather | solution.py:45
  314.6 302.9 %all-gather.6.cloned.1.call-done = bf16[16384,128]{1,0:T(8,128)(2,1)} async-done(((bf16[256,128]{1,0:T(8,128)(2,1)}), bf16[16384,128]{1,0:T(8,128)(2,1)}) %all-gather.6.cloned.1.call-update) | async-done | bytes 4194320 | tf_op jit(solution)/shard_map/all_gather | solution.py:46
  617.6 937.3 %while.17 = (s32[]{:T(128)}, f32[8,256]{1,0:T(8,128)S(1)}, f32[8,256]{1,0:T(8,128)S(1)}, f32[256,8,128]{2,0,1:T(8,128)S(1)}, s32[16384]{0:T(1024)S(1)}, /*index=...) while((s32[]{:T(128)}, f32[8,256]{1,0:T(8,128)S(1)}, ...), condition=%wide.region_7.8_spmd, body=%wide.region_1.7_spmd.sunk | while | flops 137173248 | bytes 6099561 | solution.py:64
  650.9 4.2 conditional.2
  666.0 4.2 conditional.2
  681.0 4.2 conditional.2
  696.1 4.2 conditional.2
  711.1 4.2 conditional.2
  729.5 4.2 conditional.2
  737.0 4.2 conditional.2
  752.0 4.2 conditional.2
  767.1 4.2 conditional.2
  782.1 4.2 conditional.2
  797.1 4.2 conditional.2
  812.2 4.2 conditional.2
  827.2 4.2 conditional.2
  842.3 4.2 conditional.2
  857.3 4.2 conditional.2
  872.3 4.2 conditional.2
  887.4 4.2 conditional.2
  902.4 4.2 conditional.2
  917.5 4.2 conditional.2
  932.5 4.2 conditional.2
  950.8 4.2 conditional.2
  958.4 4.2 conditional.2
  973.4 4.2 conditional.2
  988.4 4.2 conditional.2
  1003.5 4.2 conditional.2
  1018.5 4.2 conditional.2
  1033.6 4.2 conditional.2
  1112.1 4.2 conditional.2
  1183.1 4.2 conditional.2
  1190.6 4.2 conditional.2
  1205.6 4.2 conditional.2
  1220.7 4.2 conditional.2
  1235.7 4.2 conditional.2
  1250.7 4.2 conditional.2
  1265.8 4.2 conditional.2
  1280.8 4.2 conditional.2
  1295.9 4.2 conditional.2
  1310.9 4.2 conditional.2
  1325.9 4.2 conditional.2
  1341.0 4.2 conditional.2
  1356.0 4.2 conditional.2
  1371.1 4.2 conditional.2
  1389.4 4.2 conditional.2
  1400.2 4.2 conditional.2
  (1200 shorter events, 934.5 us)
Async XLA Ops:
  7.2 307.4 %all-gather.4.cloned.1.call-start = ((), (), s32[]{:S(2)}) async-start(), calls=%async_computation | async-start | bytes 4259840 | tf_op jit(solution)/shard_map/all_gather | solution.py:45
  7.9 609.6 %all-gather.6.cloned.1.call-start = ((), (), s32[]{:S(2)}) async-start(), calls=%async_computation.1 | async-start | bytes 4259840 | tf_op jit(solution)/shard_map/all_gather | solution.py:46
Sparse Core Ops, SparseCore 0:
  9.8 304.7 all-gather.3
  316.4 301.0 all-gather.5
where the time goes:
time: 1590 us; the launch traced here: 1560 us
  waiting for transfers between devices  454 us (29%)
  loops' own time  339 us (21%)
  matrix products  305 us (19%)
  other arithmetic  297 us (19%)
  blocking collectives  153 us (10%)
    another operation x1, loops' own time, shards(): state = lax.fori_loop(0, count, visit, initial)  330 us
    all_gather x1, waiting for transfers between devices, shards(): value_rows = lax.all_gather(values, 'ctx', axis=0, tiled=True)  303 us
    dot_general x122, matrix products, update(): jnp.einsum('htk,kd->thd', weights, value_block, preferred_element_type=jn...  173 us
    all_gather x1, blocking collectives, shards(): key_pos = lax.all_gather(positions, 'ctx', axis=0, tiled=True)  153 us
    all_gather x1, waiting for transfers between devices, shards(): key_rows = lax.all_gather(keys, 'ctx', axis=0, tiled=True)  150 us
    dot_general x122, matrix products, update(): jnp.einsum('thd,kd->htk', query3, key_block, preferred_element_type=jnp.f...  132 us
    and x122, other arithmetic, update(): (pos_block[None, :] <= positions[:, None]) & (pos_block < length)[None, :]  95.4 us
    reduce_min x128, other arithmetic, visit(): lowest = jnp.min(pos_block)  92.1 us
  transfers between devices with their start and end apart: 2, of which 2 were waited for; matrix products, arithmetic and copies ran while one was open for 0% of the time, Pallas kernels for 0%

commit v1 on v0

v1 whole, which is shorter than its diff:
```python
import functools
import math

import jax
import jax.numpy as jnp
from jax import lax
from jax.experimental import pallas as pl
from jax.experimental.pallas import tpu as pltpu
from jax.sharding import PartitionSpec as P

SPAN = 128
HEADS = 8
DEPTH = 128
ROWS = HEADS * SPAN
BLOCK = 4 * SPAN + 16
QROWS = 2 * SPAN + 16
ACC = DEPTH + 16
TILE = 256
TILES = ROWS // TILE
LAST = 127
UNITS = math.log2(math.e) / math.sqrt(DEPTH)
SCALE = 1.0 / math.sqrt(DEPTH)
EMPTY = -1e20
HIDDEN = -1e30
OPEN = -(1 << 20)
SHUT = 1 << 20
Y, X, Z = 2, 4, 8

f32 = jnp.float32
bf16 = jnp.bfloat16
VMEM = pl.BlockSpec(memory_space=pltpu.VMEM)
SMEM = pl.BlockSpec(memory_space=pltpu.SMEM)
ANY = pl.BlockSpec(memory_space=pl.ANY)
PARAMS = pltpu.CompilerParams(vmem_limit_bytes=48 * 2**20)


def low_rows(pos_ref):
    first, second = pos_ref[0], pos_ref[SPAN]
    return (
        pl.multiple_of(jnp.where(first < second, 0, SPAN), SPAN),
        pl.multiple_of(jnp.where(first < second, SPAN, 0), SPAN),
        lax.shift_right_logical(jnp.minimum(first, second), 7),
    )


def pack_kv_kernel(pos_ref, k_ref, v_ref, out_ref):
    low, high, run = low_rows(pos_ref)
    for i, start in enumerate((low, high)):
        out_ref[i * SPAN : (i + 1) * SPAN, :] = k_ref[pl.ds(start, SPAN), :]
        out_ref[(2 + i) * SPAN : (3 + i) * SPAN, :] = v_ref[pl.ds(start, SPAN), :].T
    out_ref[4 * SPAN :, :] = jnp.full((16, DEPTH), run.astype(f32), f32).astype(bf16)


def pack_q_kernel(pos_ref, q_ref, out_ref):
    low, high, run = low_rows(pos_ref)
    for i, start in enumerate((low, high)):
        for h in range(HEADS):
            cols = slice(h * SPAN, (h + 1) * SPAN)
            out_ref[i * SPAN : (i + 1) * SPAN, cols] = q_ref[pl.ds(start, SPAN), cols].T
    out_ref[2 * SPAN :, :] = jnp.full((16, ROWS), run.astype(f32), f32).astype(bf16)


def run_of(tile):
    return jnp.max(tile.astype(f32)).astype(jnp.int32)


def attend(sizes, pairs, refs, len_ref, qt, kv, o_ref, m_ref, s_ref, addr, base, slot_of, sems, more=()):
    q_refs, kv_refs = refs[:pairs], refs[pairs:]
    copies = []
    for i, (source, target) in enumerate(more):
        copies.append(pltpu.make_async_copy(source, target, sems.at[pairs + len(sizes) + i]))
    for i, ref in enumerate(q_refs):
        copies.append(pltpu.make_async_copy(ref, qt.at[i], sems.at[i]))
    at = 0
    for i, (ref, blocks) in enumerate(zip(kv_refs, sizes)):
        copies.append(
            pltpu.make_async_copy(ref, kv.at[pl.ds(at * BLOCK, blocks * BLOCK)], sems.at[pairs + i])
        )
        at += blocks
    total = at
    for c in copies:
        c.start()
    for c in copies:
        c.wait()

    length = len_ref[0]
    runs_q = [run_of(qt[i, 2 * SPAN : 2 * SPAN + 16, :DEPTH]) for i in range(pairs)]
    runs_k = [run_of(kv[b * BLOCK + 4 * SPAN : (b + 1) * BLOCK, :]) for b in range(total)]

    count = jnp.int32(0)

    def append(count, slot, row, first, wanted):
        addr[count] = row
        base[count] = first
        slot_of[lax.shift_right_logical(count, 1)] = slot
        return count + wanted.astype(jnp.int32)

    def pad(count, slot):
        return append(count, slot, 0, SHUT, (count & 1) == 1)

    for i in range(pairs):
        mine = runs_q[i]
        for b in range(total):
            r = runs_k[b]
            count = append(
                count, 2 * i, b * BLOCK, jnp.where(r < mine, OPEN, r * SPAN), r <= mine
            )
        count = pad(count, 2 * i)
        for b in range(total):
            count = append(count, 2 * i + 1, b * BLOCK, OPEN, jnp.bool_(True))
        for b in range(total):
            r = runs_k[b]
            first = (LAST - r) * SPAN
            full = (r > mine) & (first + SPAN <= length)
            count = append(
                count,
                2 * i + 1,
                b * BLOCK + SPAN,
                jnp.where(full, OPEN, first),
                (r >= mine) & (first < length),
            )
        count = pad(count, 2 * i + 1)
    items = lax.shift_right_logical(count, 1)

    ones = jnp.ones((16, 2 * SPAN), bf16)
    lane = lax.broadcasted_iota(jnp.int32, (1, TILE), 1) & (SPAN - 1)
    row = lax.broadcasted_iota(jnp.int32, (SPAN, 1), 0)

    def keys_at(i):
        a = pl.multiple_of(addr[2 * i], 16)
        b = pl.multiple_of(addr[2 * i + 1], 16)
        return jnp.concatenate([kv[pl.ds(a, SPAN), :], kv[pl.ds(b, SPAN), :]], 0)

    def values_at(i):
        a = pl.multiple_of(addr[2 * i] + 2 * SPAN, 16)
        b = pl.multiple_of(addr[2 * i + 1] + 2 * SPAN, 16)
        both = jnp.concatenate([kv[pl.ds(a, SPAN), :], kv[pl.ds(b, SPAN), :]], 1)
        return jnp.concatenate([both, ones], 0)

    def scores(i, t, keys):
        s = slot_of[i]
        q = qt[
            lax.shift_right_logical(s, 1),
            pl.ds(pl.multiple_of((s & 1) * SPAN, SPAN), SPAN),
            t * TILE : (t + 1) * TILE,
        ]
        return jnp.dot(keys, q, preferred_element_type=f32)

    def visit(i, cur, masked):
        slot = slot_of[i]
        values = values_at(i)
        after = jnp.minimum(i + 1, items - 1)
        keys = keys_at(after)
        if masked:
            pair = lax.shift_right_logical(slot, 1)
            mine = runs_q[0] if pairs == 1 else jnp.where(pair == 0, runs_q[0], runs_q[1])
            mine = jnp.where((slot & 1) == 1, LAST - mine, mine)
            limit = jnp.minimum(mine * SPAN + lane, length - 1)
            spots = jnp.concatenate([base[2 * i] + row, base[2 * i + 1] + row], 0)

        def weigh(t):
            s = s_ref[cur, t]
            s_ref[1 - cur, t] = scores(after, t, keys)
            if masked:
                s = jnp.where(spots <= limit, s, HIDDEN)
            cols = slice(t * TILE, (t + 1) * TILE)
            old = m_ref[slot, :, cols]
            new = jnp.maximum(old, jnp.max(s, axis=0, keepdims=True))
            m_ref[slot, :, cols] = new
            return jnp.exp2(s * UNITS - new * UNITS).astype(bf16), jnp.exp2((old - new) * UNITS)

        def gather(t, weights, factor):
            cols = slice(t * TILE, (t + 1) * TILE)
            o_ref[slot, :, cols] = o_ref[slot, :, cols] * factor + jnp.dot(
                values, weights, preferred_element_type=f32
            )

        held = None
        for t in range(TILES):
            now = weigh(t)
            if held is not None:
                gather(t - 1, *held)
            held = now
        gather(TILES - 1, *held)

    def either(i, cur):
        masked = (base[2 * i] != OPEN) | (base[2 * i + 1] != OPEN)
        pl.when(masked)(lambda: visit(i, cur, True))
        pl.when(jnp.logical_not(masked))(lambda: visit(i, cur, False))

    keys = keys_at(0)
    for t in range(TILES):
        s_ref[0, t] = scores(0, t, keys)

    def step(i, _):
        either(2 * i, 0)
        pl.when(2 * i + 1 < items)(lambda: either(2 * i + 1, 1))
        return 0

    lax.fori_loop(0, lax.shift_right_logical(items + 1, 1), step, 0)


def scratch(sizes, pairs):
    total = sum(sizes)
    room = pairs * (3 * total + 4) + 2
    return [
        pltpu.VMEM((pairs, QROWS, ROWS), bf16),
        pltpu.VMEM((total * BLOCK, DEPTH), bf16),
        pltpu.VMEM((2, TILES, 2 * SPAN, TILE), f32),
        pltpu.SMEM((room,), jnp.int32),
        pltpu.SMEM((room,), jnp.int32),
        pltpu.SMEM((room,), jnp.int32),
        pltpu.SemaphoreType.DMA((pairs + len(sizes) + 2,)),
    ]


def first_kernel(sizes, pairs, len_ref, *refs):
    given = refs[: pairs + len(sizes)]
    o_ref, m_ref, qt, kv, s_ref, addr, base, slot_of, sems = refs[pairs + len(sizes) :]
    o_ref[...] = jnp.zeros_like(o_ref)
    m_ref[...] = jnp.full_like(m_ref, EMPTY)
    attend(sizes, pairs, given, len_ref, qt, kv, o_ref, m_ref, s_ref, addr, base, slot_of, sems)


def next_kernel(sizes, pairs, len_ref, *refs):
    given = refs[: pairs + len(sizes)]
    _, _, o_ref, m_ref, qt, kv, s_ref, addr, base, slot_of, sems = refs[pairs + len(sizes) :]
    attend(sizes, pairs, given, len_ref, qt, kv, o_ref, m_ref, s_ref, addr, base, slot_of, sems)


def normal(o_ref, m_ref, slot):
    total = o_ref[slot, DEPTH : DEPTH + 1, :]
    seen = total > 0.0
    safe = jnp.where(seen, total, 1.0)
    lse = jnp.where(seen, m_ref[slot] * SCALE + jnp.log(safe), HIDDEN)
    return o_ref[slot, :DEPTH, :] * (1.0 / safe), lse


def parcel_kernel(sizes, len_ref, *refs):
    given = refs[: 1 + len(sizes)]
    o_in, m_in, out_ref, o_ref, m_ref, qt, kv, s_ref, addr, base, slot_of, sems = refs[1 + len(sizes) :]
    more = ((o_in.at[pl.ds(0, 2)], o_ref), (m_in.at[pl.ds(0, 2)], m_ref))
    attend(
        sizes, 1, given, len_ref, qt, kv, o_ref, m_ref, s_ref, addr, base, slot_of, sems, more
    )
    place = lax.broadcasted_iota(jnp.int32, (16, ROWS), 0)
    extra = jnp.zeros((16, ROWS), f32)
    for slot in range(2):
        mixed, lse = normal(o_ref, m_ref, slot)
        out_ref[slot * SPAN : (slot + 1) * SPAN, :] = mixed.astype(bf16)
        for part in range(3):
            piece = lse.astype(bf16).astype(f32)
            extra = jnp.where(place == 3 * slot + part, piece, extra)
            lse = lse - piece
    out_ref[2 * SPAN :, :] = extra.astype(bf16)


def merge_kernel(pos_ref, o_ref, m_ref, theirs_ref, out_ref, lse_ref):
    low, high, _ = low_rows(pos_ref)
    extra = theirs_ref[2 * SPAN :, :].astype(f32)
    for slot, start in enumerate((low, high)):
        mixed, lse = normal(o_ref, m_ref, slot)
        other = extra[3 * slot : 3 * slot + 1] + extra[3 * slot + 1 : 3 * slot + 2]
        other = other + extra[3 * slot + 2 : 3 * slot + 3]
        top = jnp.maximum(lse, other)
        w_own, w_other = jnp.exp(lse - top), jnp.exp(other - top)
        total = w_own + w_other
        w_own, w_other = w_own / total, w_other / total
        both = top + jnp.log(total)
        for h in range(HEADS):
            cols = slice(h * SPAN, (h + 1) * SPAN)
            block = mixed[:, cols] * w_own[:, cols] + w_other[:, cols] * theirs_ref[
                slot * SPAN : (slot + 1) * SPAN, cols
            ].astype(f32)
            out_ref[pl.ds(start, SPAN), cols] = block.T.astype(bf16)
            lse_ref[h : h + 1, pl.ds(start, SPAN)] = both[:, cols]


def cost(blocks, pairs):
    work = blocks * pairs * 2 * ROWS * SPAN
    return pl.CostEstimate(
        flops=4 * DEPTH * work, bytes_accessed=blocks * BLOCK * DEPTH * 2, transcendentals=work
    )


def state_shape(slots):
    return (
        jax.ShapeDtypeStruct((slots, ACC, ROWS), f32),
        jax.ShapeDtypeStruct((slots, 1, ROWS), f32),
    )


def count_of(arrays):
    return tuple(a.shape[0] // BLOCK for a in arrays)


def first_visit(length, queries, blocks):
    sizes, pairs = count_of(blocks), len(queries)
    return pl.pallas_call(
        functools.partial(first_kernel, sizes, pairs),
        out_shape=state_shape(2 * pairs),
        in_specs=[SMEM] + [ANY] * (pairs + len(blocks)),
        out_specs=(VMEM, VMEM),
        scratch_shapes=scratch(sizes, pairs),
        compiler_params=PARAMS,
        cost_estimate=cost(sum(sizes), pairs),
        name="first_visit",
    )(length, *queries, *blocks)


def next_visit(length, queries, blocks, state):
    sizes, pairs = count_of(blocks), len(queries)
    at = 1 + pairs + len(blocks)
    return pl.pallas_call(
        functools.partial(next_kernel, sizes, pairs),
        out_shape=state_shape(2 * pairs),
        in_specs=[SMEM] + [ANY] * (pairs + len(blocks)) + [VMEM, VMEM],
        out_specs=(VMEM, VMEM),
        input_output_aliases={at: 0, at + 1: 1},
        scratch_shapes=scratch(sizes, pairs),
        compiler_params=PARAMS,
        cost_estimate=cost(sum(sizes), pairs),
        name="next_visit",
    )(length, *queries, *blocks, *state)


def parcel_visit(length, query, blocks, state):
    sizes = count_of(blocks)
    return pl.pallas_call(
        functools.partial(parcel_kernel, sizes),
        out_shape=jax.ShapeDtypeStruct((QROWS, ROWS), bf16),
        in_specs=[SMEM] + [ANY] * (1 + len(blocks)) + [ANY, ANY],
        out_specs=VMEM,
        scratch_shapes=[pltpu.VMEM((2, ACC, ROWS), f32), pltpu.VMEM((2, 1, ROWS), f32)]
        + scratch(sizes, 1),
        compiler_params=PARAMS,
        cost_estimate=cost(sum(sizes), 1),
        name="parcel_visit",
    )(length, query, *blocks, *state)


def own_kernel(sizes, len_ref, *refs):
    given = refs[: 1 + len(sizes)]
    o_in, m_in, o_ref, m_ref, qt, kv, s_ref, addr, base, slot_of, sems = refs[1 + len(sizes) :]
    more = ((o_in.at[pl.ds(2, 2)], o_ref), (m_in.at[pl.ds(2, 2)], m_ref))
    attend(
        sizes, 1, given, len_ref, qt, kv, o_ref, m_ref, s_ref, addr, base, slot_of, sems, more
    )


def own_visit(length, query, blocks, state):
    sizes = count_of(blocks)
    return pl.pallas_call(
        functools.partial(own_kernel, sizes),
        out_shape=state_shape(2),
        in_specs=[SMEM] + [ANY] * (1 + len(blocks)) + [ANY, ANY],
        out_specs=(VMEM, VMEM),
        scratch_shapes=scratch(sizes, 1),
        compiler_params=PARAMS,
        cost_estimate=cost(sum(sizes), 1),
        name="own_visit",
    )(length, query, *blocks, *state)


def place(y, x, z):
    return ((y % Y) * X + x % X) * Z + z % Z


def send(array, dy, dx, dz):
    pairs = [
        (place(y, x, z), place(y + dy, x + dx, z + dz))
        for y in range(Y)
        for x in range(X)
        for z in range(Z)
    ]
    return lax.ppermute(array, "ctx", pairs)


def shards(queries, keys, values, positions, valid_length):
    block = pl.pallas_call(
        pack_kv_kernel,
        out_shape=jax.ShapeDtypeStruct((BLOCK, DEPTH), bf16),
        in_specs=[SMEM, VMEM, VMEM],
        out_specs=VMEM,
        name="pack_kv",
    )(positions, keys, values)
    query = pl.pallas_call(
        pack_q_kernel,
        out_shape=jax.ShapeDtypeStruct((QROWS, ROWS), bf16),
        in_specs=[SMEM, VMEM],
        out_specs=VMEM,
        name="pack_q",
    )(positions, queries)

    near = [block, send(block, 0, 1, 0), send(block, 0, -1, 0), send(block, 0, 2, 0)]
    far = [send(block, 0, 0, 3), send(block, 0, 0, -3), send(block, 0, 0, 4)]
    theirs = send(query, 1, 0, 0)
    both = [theirs, query]

    row = jnp.concatenate(near, 0)
    up, down = send(row, 0, 0, 1), send(row, 0, 0, -1)
    state = first_visit(valid_length, both, [row])

    column = jnp.concatenate(far, 0)
    side = [send(column, 0, 1, 0), send(column, 0, -1, 0), send(column, 0, 2, 0)]
    up2, down2 = send(up, 0, 0, 1), send(down, 0, 0, -1)
    state = next_visit(valid_length, both, [column, up, down], state)

    late = side + [up2, down2]
    parcel = parcel_visit(valid_length, theirs, late, state)
    back = send(parcel, 1, 0, 0)
    own, own_max = own_visit(valid_length, query, late, state)
    return pl.pallas_call(
        merge_kernel,
        out_shape=(
            jax.ShapeDtypeStruct((2 * SPAN, ROWS), bf16),
            jax.ShapeDtypeStruct((HEADS, 2 * SPAN), f32),
        ),
        in_specs=[SMEM, VMEM, VMEM, VMEM],
        out_specs=(VMEM, VMEM),
        compiler_params=PARAMS,
        name="merge",
    )(positions, own, own_max, back)


def solution(mesh):
    placed = (
        P(("dp", "ctx"), None),
        P(("dp", "ctx"), None),
        P(("dp", "ctx"), None),
        P(("dp", "ctx")),
        P("dp"),
    )
    return jax.shard_map(
        shards,
        mesh=mesh,
        in_specs=placed,
        out_specs=(P(("dp", "ctx"), None), P(None, ("dp", "ctx"))),
        check_vma=False,
    )
```

time: 1590 us -> 98.4 us (0.06)
  the two profiles are of different devices: /device:TPU:40 before, /device:TPU:36 now
where the time goes in v1:
time: 98.4 us; the launch traced here: 98.2 us
  Pallas kernels  44 us (45%)
  waiting for transfers between devices  26.3 us (27%)
  starting transfers between devices  24.4 us (25%)
  between operations  1.46 us (1%)
  local copies, waits for them, and re-layouts  1.11 us (1%)
    ppermute x15, waiting for transfers between devices, send(): return lax.ppermute(array, 'ctx', pairs)  26.3 us
    ppermute x15, starting transfers between devices, send(): return lax.ppermute(array, 'ctx', pairs)  24.4 us
    pallas_call x1, Pallas kernels, next_visit(): pl.pallas_call(functools.partial(next_kernel, sizes, pairs), out_shape=st...  12.3 us
    pallas_call x1, Pallas kernels, parcel_visit(): pl.pallas_call(functools.partial(parcel_kernel, sizes), out_shape=jax.Sha...  10.1 us
    pallas_call x1, Pallas kernels, own_visit(): pl.pallas_call(functools.partial(own_kernel, sizes), out_shape=state_shap...  9.98 us
    pallas_call x1, Pallas kernels, first_visit(): pl.pallas_call(functools.partial(first_kernel, sizes, pairs), out_shape=s...  6.22 us
    pallas_call x1, Pallas kernels, shards(): pl.pallas_call(pack_q_kernel, out_shape=jax.ShapeDtypeStruct((QROWS, ROWS...  2.06 us
  transfers between devices with their start and end apart: 15, of which 6 were waited for; matrix products, arithmetic and copies ran while one was open for 0% of the time, Pallas kernels for 31%

profile of v1, /device:TPU:36, one launch (start us, length us, event | category | flops | bytes accessed | tf_op | source)
XLA Modules:
  0.0 98.2 jit_solution(2635918278450726752)
XLA Ops:
  0.6 1.6 %pack_kv.1 = bf16[528,128]{1,0:T(8,128)(2,1)} custom-call(s32[256]{0:T(256)} %pos_ref.5, bf16[256,128]{1,0:T(8,128)(2,1)} %k_ref.1, bf16[256,128]{1,0:T(8,128)(2,1)} %v_ref.1), custom_call_target="tpu_custom_call" | custom-call | tf_op jit(solution)/shard_map/pack_kv/pallas_call | solution.py:380
  2.2 0.0 copy-start.4
  2.3 1.2 %collective-permute-start.6 = (bf16[528,128]{1,0:T(8,128)(2,1)}, bf16[528,128]{1,0:T(8,128)(2,1)S(1)}, u32[]{:S(2)}, u32[]{:S(2)}) collective-permute-start(bf16[528,128]{1,0:T(8,128)(2,1)} %pack_kv.1), channel_id=1, source_target_pairs={{0,8},{1,9},{2,10},{3,11},{4,12},{5,13},{6,14},{7,15},{8,16},{9,17... | collective-permute-start | bytes 405512 | tf_op jit(solution)/shard_map/ppermute | solution.py:376
  3.4 0.8 collective-permute-start.7
  4.3 1.7 %collective-permute-start.8 = (bf16[528,128]{1,0:T(8,128)(2,1)}, bf16[528,128]{1,0:T(8,128)(2,1)S(1)}, u32[]{:S(2)}, u32[]{:S(2)}) collective-permute-start(bf16[528,128]{1,0:T(8,128)(2,1)} %pack_kv.1), channel_id=1, source_target_pairs={{0,16},{1,17},{2,18},{3,19},{4,20},{5,21},{6,22},{7,23},{8,24},{9,... | collective-permute-start | bytes 405512 | tf_op jit(solution)/shard_map/ppermute | solution.py:376
  6.0 1.8 %collective-permute-done.6 = bf16[528,128]{1,0:T(8,128)(2,1)S(1)} collective-permute-done((bf16[528,128]{1,0:T(8,128)(2,1)}, bf16[528,128]{1,0:T(8,128)(2,1)S(1)}, u32[]{:S(2)}, u32[]{:S(2)}) %collective-permute-start.6) | collective-permute-done | bytes 135200 | tf_op jit(solution)/shard_map/ppermute | solution.py:376
  7.8 2.4 %collective-permute-done.7 = bf16[528,128]{1,0:T(8,128)(2,1)S(1)} collective-permute-done((bf16[528,128]{1,0:T(8,128)(2,1)}, bf16[528,128]{1,0:T(8,128)(2,1)S(1)}, u32[]{:S(2)}, u32[]{:S(2)}) %collective-permute-start.7) | collective-permute-done | bytes 135200 | tf_op jit(solution)/shard_map/ppermute | solution.py:376
  10.2 0.9 collective-permute-done.8
  11.0 0.9 pad_maximum_fusion.refs_2_
  11.9 2.0 %collective-permute-start.9 = (bf16[2112,128]{1,0:T(8,128)(2,1)S(1)}, bf16[2112,128]{1,0:T(8,128)(2,1)S(1)}, u32[]{:S(2)}, u32[]{:S(2)}) collective-permute-start(bf16[2112,128]{1,0:T(8,128)(2,1)S(1)} %pad_maximum_fusion.refs_2_), channel_id=1, source_target_pairs={{0,1},{1,2},{2,3},{3,4},{4,5},{5,6},{6,7},{7,0},{8,9},{9,10},{10,1... | collective-permute-start | bytes 1622024 | tf_op jit(solution)/shard_map/ppermute | solution.py:376
  13.9 0.1 collective-permute-start.11
  14.1 2.1 %pack_q.1.refs_1_.refs_0_ = bf16[272,1024]{1,0:T(8,128)(2,1)} custom-call(s32[256]{0:T(256)} %pos_ref.5, bf16[256,1024]{1,0:T(8,128)(2,1)} %q_ref.1), custom_call_target="tpu_custom_call" | custom-call | tf_op jit(solution)/shard_map/pack_q/pallas_call | solution.py:387
  16.1 1.6 %collective-permute-start.13 = (bf16[272,1024]{1,0:T(8,128)(2,1)}, bf16[272,1024]{1,0:T(8,128)(2,1)S(1)}, u32[]{:S(2)}, u32[]{:S(2)}) collective-permute-start(bf16[272,1024]{1,0:T(8,128)(2,1)} %pack_q.1.refs_1_.refs_0_), channel_id=1, source_target_pairs={{0,32},{1,33},{2,34},{3,35},{4,36},{5,37},{6,38},{7,39},{8,40},{9,... | collective-permute-start | bytes 1671176 | tf_op jit(solution)/shard_map/ppermute | solution.py:376
  17.7 0.0 copy-done.4
  17.7 7.0 %collective-permute-start = (bf16[528,128]{1,0:T(8,128)(2,1)S(1)}, bf16[528,128]{1,0:T(8,128)(2,1)S(1)}, u32[]{:S(2)}, u32[]{:S(2)}) collective-permute-start(bf16[528,128]{1,0:T(8,128)(2,1)S(1)} %copy-done.4), channel_id=1, source_target_pairs={{0,3},{1,4},{2,5},{3,6},{4,7},{5,0},{6,1},{7,2},{8,11},{9,12},{10,... | collective-permute-start | bytes 405512 | tf_op jit(solution)/shard_map/ppermute | solution.py:376
  24.7 0.0 collective-permute-start.1
  24.7 14.2 %collective-permute-done = bf16[528,128]{1,0:T(8,128)(2,1)S(1)} collective-permute-done((bf16[528,128]{1,0:T(8,128)(2,1)S(1)}, bf16[528,128]{1,0:T(8,128)(2,1)S(1)}, u32[]{:S(2)}, u32[]{:S(2)}) %collective-permute-start) | collective-permute-done | bytes 135200 | tf_op jit(solution)/shard_map/ppermute | solution.py:376
  38.9 0.5 collective-permute-start.2
  39.5 0.0 collective-permute-done.9.refs_3_
  39.5 3.2 %collective-permute-start.10 = (bf16[2112,128]{1,0:T(8,128)(2,1)S(1)}, bf16[2112,128]{1,0:T(8,128)(2,1)S(1)}, u32[]{:S(2)}, u32[]{:S(2)}) collective-permute-start(bf16[2112,128]{1,0:T(8,128)(2,1)S(1)} %collective-permute-done.9.refs_3_), channel_id=1, source_target_pairs={{0,1},{1,2},{2,3},{3,4},{4,5},{5,6},{6,7},{7,0},{8,9},{9,10},{10,1... | collective-permute-start | bytes 1622024 | tf_op jit(solution)/shard_map/ppermute | solution.py:376
  42.7 0.0 collective-permute-done.11.refs_4_
  42.7 0.0 collective-permute-start.12
  42.7 0.7 collective-permute-done.1
  43.4 6.5 %collective-permute-done.2 = bf16[528,128]{1,0:T(8,128)(2,1)S(1)} collective-permute-done((bf16[528,128]{1,0:T(8,128)(2,1)S(1)}, bf16[528,128]{1,0:T(8,128)(2,1)S(1)}, u32[]{:S(2)}, u32[]{:S(2)}) %collective-permute-start.2) | collective-permute-done | bytes 135200 | tf_op jit(solution)/shard_map/ppermute | solution.py:376
  49.9 2.9 %collective-permute-start.3 = (bf16[1584,128]{1,0:T(8,128)(2,1)S(1)}, bf16[1584,128]{1,0:T(8,128)(2,1)S(1)}, u32[]{:S(2)}, u32[]{:S(2)}) collective-permute-start(bf16[1584,128]{1,0:T(8,128)(2,1)S(1)} %constant_dynamic-update-slice_fusion.refs_2_), channel_id=1, source_target_pairs={{0,8},{1,9},{2,10},{3,11},{4,12},{5,13},{6,14},{7,15},{8,16},{9,17... | collective-permute-start | bytes 1216520 | tf_op jit(solution)/shard_map/ppermute | solution.py:376
  52.8 0.0 collective-permute-start.4
  52.8 0.0 collective-permute-done.13.refs_0_
  52.8 3.1 %collective-permute-start.5 = (bf16[1584,128]{1,0:T(8,128)(2,1)S(1)}, bf16[1584,128]{1,0:T(8,128)(2,1)S(1)}, u32[]{:S(2)}, u32[]{:S(2)}) collective-permute-start(bf16[1584,128]{1,0:T(8,128)(2,1)S(1)} %constant_dynamic-update-slice_fusion.refs_2_), channel_id=1, source_target_pairs={{0,16},{1,17},{2,18},{3,19},{4,20},{5,21},{6,22},{7,23},{8,24},{9,... | collective-permute-start | bytes 1216520 | tf_op jit(solution)/shard_map/ppermute | solution.py:376
  56.6 0.0 copy-start
  56.6 1.0 %copy-done = bf16[272,1024]{1,0:T(8,128)(2,1)S(1)} copy-done((bf16[272,1024]{1,0:T(8,128)(2,1)S(1)}, bf16[272,1024]{1,0:T(8,128)(2,1)}, u32[]{:S(2)}) %copy-start) | copy-done | bytes 557080
  57.6 6.2 %first_visit.1 = (f32[4,144,1024]{2,1,0:T(8,128)S(1)}, f32[4,1,1024]{2,1,0:T(1,128)S(1)}) custom-call(s32[1]{0:T(128)S(6)} %copy.13.len_ref, bf16[272,1024]{1,0:T(8,128)(2,1)S(1)} %collective-permute-done.13.refs_0_, bf16[272,1024]{1,0:T(8,128)(2,1)S(1)} %copy-done, bf16[2112,128]{1,0:T(8,128)(2,1)S(1)} %pad_maximum_fusion.refs_2_), custom_call_target="tpu_custom_call" | custom-call | flops 1073741824 | bytes 540672 | tf_op jit(solution)/shard_map/first_visit/pallas_call | solution.py:299
  63.9 12.3 %next_visit.1 = (f32[4,144,1024]{2,1,0:T(8,128)S(1)}, f32[4,1,1024]{2,1,0:T(1,128)S(1)}) custom-call(s32[1]{0:T(128)S(6)} %copy.13.len_ref, bf16[272,1024]{1,0:T(8,128)(2,1)S(1)} %collective-permute-done.13.refs_0_, bf16[272,1024]{1,0:T(8,128)(2,1)S(1)} %copy-done, ...), custom_call_target="tpu_custom_call", output_to_operand_aliasing={{0}: (6, {}), {1}: (7, {})} | custom-call | flops 2952790016 | bytes 1486848 | tf_op jit(solution)/shard_map/next_visit/pallas_call | solution.py:314
  76.2 0.0 copy-start.3
  76.2 0.0 collective-permute-done.3.refs_1_
  76.2 0.0 collective-permute-done.4.refs_2_
  76.2 0.0 collective-permute-done.5.refs_3_
  76.2 0.0 collective-permute-done.10.refs_4_
  76.3 0.0 collective-permute-done.12.refs_5_
  76.3 0.0 copy-start.1
  76.3 10.1 %parcel_visit.1 = bf16[272,1024]{1,0:T(8,128)(2,1)S(1)} custom-call(s32[1]{0:T(128)S(6)} %copy.13.len_ref, bf16[272,1024]{1,0:T(8,128)(2,1)S(1)} %collective-permute-done.13.refs_0_, bf16[1584,128]{1,0:T(8,128)(2,1)S(1)} %collective-permute-done.3.refs_1_, bf16[1584,128]{1,0:T(8,128)(2,1)S(1)} %collective-permute-done.4.refs_2_, ...), custom_call_target="tpu_custom_call" | custom-call | flops 2281701376 | bytes 2297856 | tf_op jit(solution)/shard_map/parcel_visit/pallas_call | solution.py:329
  86.3 0.0 copy-done.3
  86.4 0.0 copy-start.2
  86.4 0.1 collective-permute-start.14
  86.5 0.0 copy-done.1
  86.5 10.0 %own_visit.1 = (f32[2,144,1024]{2,1,0:T(8,128)S(1)}, f32[2,1,1024]{2,1,0:T(1,128)S(1)}) custom-call(s32[1]{0:T(128)S(6)} %copy.13.len_ref, bf16[272,1024]{1,0:T(8,128)(2,1)S(1)} %copy-done.1, bf16[1584,128]{1,0:T(8,128)(2,1)S(1)} %collective-permute-done.3.refs_1_, bf16[1584,128]{1,0:T(8,128)(2,1)S(1)} %collective-permute-done.4.refs_2_, ...), custom_call_target="tpu_custom_call" | custom-call | flops 2281701376 | bytes 2297856 | tf_op jit(solution)/shard_map/own_visit/pallas_call | solution.py:353
  96.5 0.0 collective-permute-done.14.theirs_ref
  96.5 0.0 copy-done.2
  96.5 1.7 %merge.1 = (bf16[256,1024]{1,0:T(8,128)(2,1)}, f32[8,256]{1,0:T(8,128)}) custom-call(s32[256]{0:T(256)S(1)} %copy-done.2, f32[2,144,1024]{2,1,0:T(8,128)S(1)} %get-tuple-element.12.o_ref, f32[2,1,1024]{2,1,0:T(1,128)S(1)} %get-tuple-element.13.m_ref, bf16[272,1024]{1,0:T(8,128)(2,1)S(1)} %collective-permute-done.14.theirs_ref), custom_call_target="tpu_custom_call" | custom-call | tf_op jit(solution)/shard_map/merge/pallas_call | solution.py:413
  (3 shorter events, 0.0 us)
Async XLA Ops:
  2.2 15.4 %copy-start.4 = (bf16[528,128]{1,0:T(8,128)(2,1)S(1)}, bf16[528,128]{1,0:T(8,128)(2,1)}, u32[]{:S(2)}) copy-start(bf16[528,128]{1,0:T(8,128)(2,1)} %pack_kv.1) | copy-start | bytes 405508
  2.3 5.5 %collective-permute-start.6 = (bf16[528,128]{1,0:T(8,128)(2,1)}, bf16[528,128]{1,0:T(8,128)(2,1)S(1)}, u32[]{:S(2)}, u32[]{:S(2)}) collective-permute-start(bf16[528,128]{1,0:T(8,128)(2,1)} %pack_kv.1), channel_id=1, source_target_pairs={{0,8},{1,9},{2,10},{3,11},{4,12},{5,13},{6,14},{7,15},{8,16},{9,17... | collective-permute-start | bytes 405512 | tf_op jit(solution)/shard_map/ppermute | solution.py:376
  3.4 6.7 %collective-permute-start.7 = (bf16[528,128]{1,0:T(8,128)(2,1)}, bf16[528,128]{1,0:T(8,128)(2,1)S(1)}, u32[]{:S(2)}, u32[]{:S(2)}) collective-permute-start(bf16[528,128]{1,0:T(8,128)(2,1)} %pack_kv.1), channel_id=1, source_target_pairs={{0,24},{1,25},{2,26},{3,27},{4,28},{5,29},{6,30},{7,31},{8,0},{9,1... | collective-permute-start | bytes 405512 | tf_op jit(solution)/shard_map/ppermute | solution.py:376
  4.3 6.7 %collective-permute-start.8 = (bf16[528,128]{1,0:T(8,128)(2,1)}, bf16[528,128]{1,0:T(8,128)(2,1)S(1)}, u32[]{:S(2)}, u32[]{:S(2)}) collective-permute-start(bf16[528,128]{1,0:T(8,128)(2,1)} %pack_kv.1), channel_id=1, source_target_pairs={{0,16},{1,17},{2,18},{3,19},{4,20},{5,21},{6,22},{7,23},{8,24},{9,... | collective-permute-start | bytes 405512 | tf_op jit(solution)/shard_map/ppermute | solution.py:376
  11.9 27.5 %collective-permute-start.9 = (bf16[2112,128]{1,0:T(8,128)(2,1)S(1)}, bf16[2112,128]{1,0:T(8,128)(2,1)S(1)}, u32[]{:S(2)}, u32[]{:S(2)}) collective-permute-start(bf16[2112,128]{1,0:T(8,128)(2,1)S(1)} %pad_maximum_fusion.refs_2_), channel_id=1, source_target_pairs={{0,1},{1,2},{2,3},{3,4},{4,5},{5,6},{6,7},{7,0},{8,9},{9,10},{10,1... | collective-permute-start | bytes 1622024 | tf_op jit(solution)/shard_map/ppermute | solution.py:376
  13.9 28.8 %collective-permute-start.11 = (bf16[2112,128]{1,0:T(8,128)(2,1)S(1)}, bf16[2112,128]{1,0:T(8,128)(2,1)S(1)}, u32[]{:S(2)}, u32[]{:S(2)}) collective-permute-start(bf16[2112,128]{1,0:T(8,128)(2,1)S(1)} %pad_maximum_fusion.refs_2_), channel_id=1, source_target_pairs={{0,7},{1,0},{2,1},{3,2},{4,3},{5,4},{6,5},{7,6},{8,15},{9,8},{10,9... | collective-permute-start | bytes 1622024 | tf_op jit(solution)/shard_map/ppermute | solution.py:376
  16.1 36.7 %collective-permute-start.13 = (bf16[272,1024]{1,0:T(8,128)(2,1)}, bf16[272,1024]{1,0:T(8,128)(2,1)S(1)}, u32[]{:S(2)}, u32[]{:S(2)}) collective-permute-start(bf16[272,1024]{1,0:T(8,128)(2,1)} %pack_q.1.refs_1_.refs_0_), channel_id=1, source_target_pairs={{0,32},{1,33},{2,34},{3,35},{4,36},{5,37},{6,38},{7,39},{8,40},{9,... | collective-permute-start | bytes 1671176 | tf_op jit(solution)/shard_map/ppermute | solution.py:376
  17.7 21.2 %collective-permute-start = (bf16[528,128]{1,0:T(8,128)(2,1)S(1)}, bf16[528,128]{1,0:T(8,128)(2,1)S(1)}, u32[]{:S(2)}, u32[]{:S(2)}) collective-permute-start(bf16[528,128]{1,0:T(8,128)(2,1)S(1)} %copy-done.4), channel_id=1, source_target_pairs={{0,3},{1,4},{2,5},{3,6},{4,7},{5,0},{6,1},{7,2},{8,11},{9,12},{10,... | collective-permute-start | bytes 405512 | tf_op jit(solution)/shard_map/ppermute | solution.py:376
  24.7 18.6 %collective-permute-start.1 = (bf16[528,128]{1,0:T(8,128)(2,1)S(1)}, bf16[528,128]{1,0:T(8,128)(2,1)S(1)}, u32[]{:S(2)}, u32[]{:S(2)}) collective-permute-start(bf16[528,128]{1,0:T(8,128)(2,1)S(1)} %copy-done.4), channel_id=1, source_target_pairs={{0,5},{1,6},{2,7},{3,0},{4,1},{5,2},{6,3},{7,4},{8,13},{9,14},{10,... | collective-permute-start | bytes 405512 | tf_op jit(solution)/shard_map/ppermute | solution.py:376
  38.9 10.9 %collective-permute-start.2 = (bf16[528,128]{1,0:T(8,128)(2,1)S(1)}, bf16[528,128]{1,0:T(8,128)(2,1)S(1)}, u32[]{:S(2)}, u32[]{:S(2)}) collective-permute-start(bf16[528,128]{1,0:T(8,128)(2,1)S(1)} %copy-done.4), channel_id=1, source_target_pairs={{0,4},{1,5},{2,6},{3,7},{4,0},{5,1},{6,2},{7,3},{8,12},{9,13},{10,... | collective-permute-start | bytes 405512 | tf_op jit(solution)/shard_map/ppermute | solution.py:376
  39.5 36.8 %collective-permute-start.10 = (bf16[2112,128]{1,0:T(8,128)(2,1)S(1)}, bf16[2112,128]{1,0:T(8,128)(2,1)S(1)}, u32[]{:S(2)}, u32[]{:S(2)}) collective-permute-start(bf16[2112,128]{1,0:T(8,128)(2,1)S(1)} %collective-permute-done.9.refs_3_), channel_id=1, source_target_pairs={{0,1},{1,2},{2,3},{3,4},{4,5},{5,6},{6,7},{7,0},{8,9},{9,10},{10,1... | collective-permute-start | bytes 1622024 | tf_op jit(solution)/shard_map/ppermute | solution.py:376
  42.7 33.5 %collective-permute-start.12 = (bf16[2112,128]{1,0:T(8,128)(2,1)S(1)}, bf16[2112,128]{1,0:T(8,128)(2,1)S(1)}, u32[]{:S(2)}, u32[]{:S(2)}) collective-permute-start(bf16[2112,128]{1,0:T(8,128)(2,1)S(1)} %collective-permute-done.11.refs_4_), channel_id=1, source_target_pairs={{0,7},{1,0},{2,1},{3,2},{4,3},{5,4},{6,5},{7,6},{8,15},{9,8},{10,9... | collective-permute-start | bytes 1622024 | tf_op jit(solution)/shard_map/ppermute | solution.py:376
  49.9 26.3 %collective-permute-start.3 = (bf16[1584,128]{1,0:T(8,128)(2,1)S(1)}, bf16[1584,128]{1,0:T(8,128)(2,1)S(1)}, u32[]{:S(2)}, u32[]{:S(2)}) collective-permute-start(bf16[1584,128]{1,0:T(8,128)(2,1)S(1)} %constant_dynamic-update-slice_fusion.refs_2_), channel_id=1, source_target_pairs={{0,8},{1,9},{2,10},{3,11},{4,12},{5,13},{6,14},{7,15},{8,16},{9,17... | collective-permute-start | bytes 1216520 | tf_op jit(solution)/shard_map/ppermute | solution.py:376
  52.8 23.4 %collective-permute-start.4 = (bf16[1584,128]{1,0:T(8,128)(2,1)S(1)}, bf16[1584,128]{1,0:T(8,128)(2,1)S(1)}, u32[]{:S(2)}, u32[]{:S(2)}) collective-permute-start(bf16[1584,128]{1,0:T(8,128)(2,1)S(1)} %constant_dynamic-update-slice_fusion.refs_2_), channel_id=1, source_target_pairs={{0,24},{1,25},{2,26},{3,27},{4,28},{5,29},{6,30},{7,31},{8,0},{9,1... | collective-permute-start | bytes 1216520 | tf_op jit(solution)/shard_map/ppermute | solution.py:376
  52.8 23.4 %collective-permute-start.5 = (bf16[1584,128]{1,0:T(8,128)(2,1)S(1)}, bf16[1584,128]{1,0:T(8,128)(2,1)S(1)}, u32[]{:S(2)}, u32[]{:S(2)}) collective-permute-start(bf16[1584,128]{1,0:T(8,128)(2,1)S(1)} %constant_dynamic-update-slice_fusion.refs_2_), channel_id=1, source_target_pairs={{0,16},{1,17},{2,18},{3,19},{4,20},{5,21},{6,22},{7,23},{8,24},{9,... | collective-permute-start | bytes 1216520 | tf_op jit(solution)/shard_map/ppermute | solution.py:376
  56.6 1.1 %copy-start = (bf16[272,1024]{1,0:T(8,128)(2,1)S(1)}, bf16[272,1024]{1,0:T(8,128)(2,1)}, u32[]{:S(2)}) copy-start(bf16[272,1024]{1,0:T(8,128)(2,1)} %pack_q.1.refs_1_.refs_0_) | copy-start | bytes 1671172
  76.2 10.1 %copy-start.3 = (f32[4,144,1024]{2,1,0:T(8,128)}, f32[4,144,1024]{2,1,0:T(8,128)S(1)}, u32[]{:S(2)}) copy-start(f32[4,144,1024]{2,1,0:T(8,128)S(1)} %get-tuple-element.10.refs_6_) | copy-start | bytes 7077892
  76.3 10.2 %copy-start.1 = (bf16[272,1024]{1,0:T(8,128)(2,1)S(1)}, bf16[272,1024]{1,0:T(8,128)(2,1)}, u32[]{:S(2)}) copy-start(bf16[272,1024]{1,0:T(8,128)(2,1)} %pack_q.1.refs_1_.refs_0_) | copy-start | bytes 1671172
  86.4 10.1 %copy-start.2 = (s32[256]{0:T(256)S(1)}, s32[256]{0:T(256)}, u32[]{:S(2)}) copy-start(s32[256]{0:T(256)} %pos_ref.5) | copy-start | bytes 3076
  86.4 10.1 %collective-permute-start.14 = (bf16[272,1024]{1,0:T(8,128)(2,1)S(1)}, bf16[272,1024]{1,0:T(8,128)(2,1)S(1)}, u32[]{:S(2)}, u32[]{:S(2)}) collective-permute-start(bf16[272,1024]{1,0:T(8,128)(2,1)S(1)} %parcel_visit.1), channel_id=1, source_target_pairs={{0,32},{1,33},{2,34},{3,35},{4,36},{5,37},{6,38},{7,39},{8,40},{9,... | collective-permute-start | bytes 1671176 | tf_op jit(solution)/shard_map/ppermute | solution.py:376

commit v2 on v1

v2 whole, which is shorter than its diff:
```python
import functools
import math

import jax
import jax.numpy as jnp
from jax import lax
from jax.experimental import pallas as pl
from jax.experimental.pallas import tpu as pltpu
from jax.sharding import PartitionSpec as P

SPAN = 128
HEADS = 8
DEPTH = 128
ROWS = HEADS * SPAN
BLOCK = 4 * SPAN + 16
QROWS = 2 * SPAN + 16
ACC = DEPTH + 16
TILE = 256
TILES = ROWS // TILE
LAST = 127
UNITS = math.log2(math.e) / math.sqrt(DEPTH)
SCALE = 1.0 / math.sqrt(DEPTH)
EMPTY = -1e20
HIDDEN = -1e30
OPEN = -(1 << 20)
SHUT = 1 << 20
Y, X, Z = 2, 4, 8

f32 = jnp.float32
bf16 = jnp.bfloat16
VMEM = pl.BlockSpec(memory_space=pltpu.VMEM)
SMEM = pl.BlockSpec(memory_space=pltpu.SMEM)
ANY = pl.BlockSpec(memory_space=pl.ANY)
PARAMS = pltpu.CompilerParams(vmem_limit_bytes=48 * 2**20)


def low_rows(pos_ref):
    first, second = pos_ref[0], pos_ref[SPAN]
    return (
        pl.multiple_of(jnp.where(first < second, 0, SPAN), SPAN),
        pl.multiple_of(jnp.where(first < second, SPAN, 0), SPAN),
        lax.shift_right_logical(jnp.minimum(first, second), 7),
    )


def pack_kv_kernel(pos_ref, k_ref, v_ref, out_ref):
    low, high, run = low_rows(pos_ref)
    for i, start in enumerate((low, high)):
        out_ref[i * SPAN : (i + 1) * SPAN, :] = k_ref[pl.ds(start, SPAN), :]
        out_ref[(2 + i) * SPAN : (3 + i) * SPAN, :] = v_ref[pl.ds(start, SPAN), :].T
    out_ref[4 * SPAN :, :] = jnp.full((16, DEPTH), run.astype(f32), f32).astype(bf16)


def pack_q_kernel(pos_ref, q_ref, out_ref, copy_ref):
    low, high, run = low_rows(pos_ref)
    for i, start in enumerate((low, high)):
        for h in range(HEADS):
            cols = slice(h * SPAN, (h + 1) * SPAN)
            out_ref[i * SPAN : (i + 1) * SPAN, cols] = q_ref[pl.ds(start, SPAN), cols].T
    out_ref[2 * SPAN :, :] = jnp.full((16, ROWS), run.astype(f32), f32).astype(bf16)
    copy_ref[...] = out_ref[...]


def run_of(tile):
    return jnp.max(tile.astype(f32)).astype(jnp.int32)


def attend(sizes, kv_refs, kv, len_ref, q_ref, state, work, sems, fetch=True):
    o_ref, m_ref = state
    s_ref, addr, base, slot_of = work
    total = sum(sizes)
    if fetch and kv_refs is not None:
        copies = []
        at = 0
        for i, (ref, blocks) in enumerate(zip(kv_refs, sizes)):
            copies.append(
                pltpu.make_async_copy(ref, kv.at[pl.ds(at * BLOCK, blocks * BLOCK)], sems.at[i])
            )
            at += blocks
        for c in copies:
            c.start()
        for c in copies:
            c.wait()

    length = len_ref[0]
    mine = run_of(q_ref[2 * SPAN : 2 * SPAN + 16, :DEPTH])
    seen = range(total)
    runs = {b: run_of(kv[b * BLOCK + 4 * SPAN : (b + 1) * BLOCK, :]) for b in seen}

    def append(count, slot, row, first, wanted):
        addr[count] = row
        base[count] = first
        slot_of[lax.shift_right_logical(count, 1)] = slot
        return count + wanted.astype(jnp.int32)

    def pad(count, slot):
        return append(count, slot, 0, SHUT, (count & 1) == 1)

    count = jnp.int32(0)
    for b in seen:
        r = runs[b]
        count = append(count, 0, b * BLOCK, jnp.where(r < mine, OPEN, r * SPAN), r <= mine)
    count = pad(count, 0)
    for b in seen:
        count = append(count, 1, b * BLOCK, OPEN, jnp.bool_(True))
    for b in seen:
        r = runs[b]
        first = (LAST - r) * SPAN
        full = (r > mine) & (first + SPAN <= length)
        count = append(
            count,
            1,
            b * BLOCK + SPAN,
            jnp.where(full, OPEN, first),
            (r >= mine) & (first < length),
        )
    count = pad(count, 1)
    items = lax.shift_right_logical(count, 1)

    ones = jnp.ones((16, 2 * SPAN), bf16)
    lane = lax.broadcasted_iota(jnp.int32, (1, TILE), 1) & (SPAN - 1)
    row = lax.broadcasted_iota(jnp.int32, (SPAN, 1), 0)

    def keys_at(i):
        a = pl.multiple_of(addr[2 * i], 16)
        b = pl.multiple_of(addr[2 * i + 1], 16)
        return jnp.concatenate([kv[pl.ds(a, SPAN), :], kv[pl.ds(b, SPAN), :]], 0)

    def values_at(i):
        a = pl.multiple_of(addr[2 * i] + 2 * SPAN, 16)
        b = pl.multiple_of(addr[2 * i + 1] + 2 * SPAN, 16)
        both = jnp.concatenate([kv[pl.ds(a, SPAN), :], kv[pl.ds(b, SPAN), :]], 1)
        return jnp.concatenate([both, ones], 0)

    def scores(i, t, keys):
        start = pl.multiple_of(slot_of[i] * SPAN, SPAN)
        q = q_ref[pl.ds(start, SPAN), t * TILE : (t + 1) * TILE]
        return jnp.dot(keys, q, preferred_element_type=f32)

    def visit(i, cur, masked):
        slot = slot_of[i]
        values = values_at(i)
        after = jnp.minimum(i + 1, items - 1)
        keys = keys_at(after)
        if masked:
            run = jnp.where(slot == 1, LAST - mine, mine)
            limit = jnp.minimum(run * SPAN + lane, length - 1)
            spots = jnp.concatenate([base[2 * i] + row, base[2 * i + 1] + row], 0)

        def weigh(t):
            s = s_ref[cur, t]
            s_ref[1 - cur, t] = scores(after, t, keys)
            if masked:
                s = jnp.where(spots <= limit, s, HIDDEN)
            cols = slice(t * TILE, (t + 1) * TILE)
            old = m_ref[slot, :, cols]
            new = jnp.maximum(old, jnp.max(s, axis=0, keepdims=True))
            m_ref[slot, :, cols] = new
            return jnp.exp2(s * UNITS - new * UNITS).astype(bf16), jnp.exp2((old - new) * UNITS)

        def gather(t, weights, factor):
            cols = slice(t * TILE, (t + 1) * TILE)
            o_ref[slot, :, cols] = o_ref[slot, :, cols] * factor + jnp.dot(
                values, weights, preferred_element_type=f32
            )

        held = None
        for t in range(TILES):
            now = weigh(t)
            if held is not None:
                gather(t - 1, *held)
            held = now
        gather(TILES - 1, *held)

    def either(i, cur):
        masked = (base[2 * i] != OPEN) | (base[2 * i + 1] != OPEN)
        pl.when(masked)(lambda: visit(i, cur, True))
        pl.when(jnp.logical_not(masked))(lambda: visit(i, cur, False))

    keys = keys_at(0)
    for t in range(TILES):
        s_ref[0, t] = scores(0, t, keys)

    def step(i, _):
        either(2 * i, 0)
        pl.when(2 * i + 1 < items)(lambda: either(2 * i + 1, 1))
        return 0

    lax.fori_loop(0, lax.shift_right_logical(items + 1, 1), step, 0)


def scratch(sizes):
    total = sum(sizes)
    room = 3 * total + 6
    return [
        pltpu.VMEM((total * BLOCK, DEPTH), bf16),
        pltpu.SemaphoreType.DMA((len(sizes),)),
        pltpu.VMEM((2, TILES, 2 * SPAN, TILE), f32),
        pltpu.SMEM((room,), jnp.int32),
        pltpu.SMEM((room,), jnp.int32),
        pltpu.SMEM((room,), jnp.int32),
    ]


def blank(o_ref, m_ref):
    o_ref[...] = jnp.zeros_like(o_ref)
    m_ref[...] = jnp.full_like(m_ref, EMPTY)


def first_kernel(sizes, len_ref, q_ref, kv, o_ref, m_ref, s_ref, addr, base, slot_of):
    blank(o_ref, m_ref)
    work = (s_ref, addr, base, slot_of)
    attend(sizes, None, kv, len_ref, q_ref, (o_ref, m_ref), work, None)


def join_kernel(sizes, len_ref, q_ref, *refs):
    n = len(sizes)
    o_ref, m_ref, kv, sems, *work = refs[n:]
    blank(o_ref, m_ref)
    attend(sizes, refs[:n], kv, len_ref, q_ref, (o_ref, m_ref), work, sems)


def both_kernel(sizes, len_ref, theirs_ref, q_ref, *refs):
    n = len(sizes)
    _, _, _, _, o1, m1, o2, m2, kv, sems, *work = refs[n:]
    attend(sizes, refs[:n], kv, len_ref, theirs_ref, (o1, m1), work, sems)
    attend(sizes, refs[:n], kv, len_ref, q_ref, (o2, m2), work, sems, False)


def one_kernel(sizes, len_ref, q_ref, *refs):
    n = len(sizes)
    _, _, o_ref, m_ref, kv, sems, *work = refs[n:]
    attend(sizes, refs[:n], kv, len_ref, q_ref, (o_ref, m_ref), work, sems)


def normal(o_ref, m_ref, slot):
    total = o_ref[slot, DEPTH : DEPTH + 1, :]
    seen = total > 0.0
    safe = jnp.where(seen, total, 1.0)
    lse = jnp.where(seen, m_ref[slot] * SCALE + jnp.log(safe), HIDDEN)
    return o_ref[slot, :DEPTH, :] * (1.0 / safe), lse


def parcel_kernel(sizes, len_ref, q_ref, *refs):
    n = len(sizes)
    _, _, o_ref, m_ref, out_ref, kv, sems, *work = refs[n:]
    attend(sizes, refs[:n], kv, len_ref, q_ref, (o_ref, m_ref), work, sems)
    place = lax.broadcasted_iota(jnp.int32, (16, ROWS), 0)
    extra = jnp.zeros((16, ROWS), f32)
    for slot in range(2):
        mixed, lse = normal(o_ref, m_ref, slot)
        out_ref[slot * SPAN : (slot + 1) * SPAN, :] = mixed.astype(bf16)
        for part in range(3):
            piece = lse.astype(bf16).astype(f32)
            extra = jnp.where(place == 3 * slot + part, piece, extra)
            lse = lse - piece
    out_ref[2 * SPAN :, :] = extra.astype(bf16)


def merge_kernel(pos_ref, o_ref, m_ref, theirs_ref, out_ref, lse_ref):
    low, high, _ = low_rows(pos_ref)
    extra = theirs_ref[2 * SPAN :, :].astype(f32)
    for slot, start in enumerate((low, high)):
        mixed, lse = normal(o_ref, m_ref, slot)
        other = extra[3 * slot : 3 * slot + 1] + extra[3 * slot + 1 : 3 * slot + 2]
        other = other + extra[3 * slot + 2 : 3 * slot + 3]
        top = jnp.maximum(lse, other)
        w_own, w_other = jnp.exp(lse - top), jnp.exp(other - top)
        total = w_own + w_other
        w_own, w_other = w_own / total, w_other / total
        both = top + jnp.log(total)
        for h in range(HEADS):
            cols = slice(h * SPAN, (h + 1) * SPAN)
            block = mixed[:, cols] * w_own[:, cols] + w_other[:, cols] * theirs_ref[
                slot * SPAN : (slot + 1) * SPAN, cols
            ].astype(f32)
            out_ref[pl.ds(start, SPAN), cols] = block.T.astype(bf16)
            lse_ref[h : h + 1, pl.ds(start, SPAN)] = both[:, cols]


def cost(blocks, pairs):
    work = blocks * pairs * 2 * ROWS * SPAN
    return pl.CostEstimate(
        flops=20 * DEPTH * work, bytes_accessed=blocks * BLOCK * DEPTH * 2, transcendentals=work
    )


STATE = (
    jax.ShapeDtypeStruct((2, ACC, ROWS), f32),
    jax.ShapeDtypeStruct((2, 1, ROWS), f32),
)


def count_of(arrays):
    return tuple(a.shape[0] // BLOCK for a in arrays)


def visit(kernel, name, length, queries, blocks, given=(), shapes=STATE, pairs=None):
    sizes = count_of(blocks)
    at = 1 + len(queries) + len(blocks)
    alone = kernel is first_kernel
    spare = len(shapes) - len(given)
    shift = 0 if kernel is parcel_kernel else spare
    room = scratch(sizes)
    return pl.pallas_call(
        functools.partial(kernel, sizes),
        out_shape=shapes,
        in_specs=[SMEM] + [VMEM] * len(queries) + [VMEM if alone else ANY] * len(blocks) + [VMEM] * len(given),
        out_specs=(VMEM,) * len(shapes),
        input_output_aliases={at + i: shift + i for i in range(len(given))},
        scratch_shapes=room[2:] if alone else room,
        compiler_params=PARAMS,
        cost_estimate=cost(sum(sizes), pairs or len(queries)),
        name=name,
    )(length, *queries, *blocks, *given)


def place(y, x, z):
    return ((y % Y) * X + x % X) * Z + z % Z


def send(array, dy, dx, dz):
    pairs = [
        (place(y, x, z), place(y + dy, x + dx, z + dz))
        for y in range(Y)
        for x in range(X)
        for z in range(Z)
    ]
    return lax.ppermute(array, "ctx", pairs)


def shards(queries, keys, values, positions, valid_length):
    block = pl.pallas_call(
        pack_kv_kernel,
        out_shape=jax.ShapeDtypeStruct((BLOCK, DEPTH), bf16),
        in_specs=[SMEM, VMEM, VMEM],
        out_specs=VMEM,
        name="pack_kv",
    )(positions, keys, values)
    query, outgoing = pl.pallas_call(
        pack_q_kernel,
        out_shape=(pltpu.VMEM((QROWS, ROWS), bf16), jax.ShapeDtypeStruct((QROWS, ROWS), bf16)),
        in_specs=[SMEM, VMEM],
        out_specs=(VMEM, VMEM),
        name="pack_q",
    )(positions, queries)

    near = [block, send(block, 0, 1, 0), send(block, 0, -1, 0), send(block, 0, 2, 0)]
    far = [send(block, 0, 0, 4), send(block, 0, 0, 3), send(block, 0, 0, -3)]
    theirs = send(outgoing, 1, 0, 0)

    row = jnp.concatenate(near, 0)
    up, down = send(row, 0, 0, 1), send(row, 0, 0, -1)
    own = visit(first_kernel, "first_visit", valid_length, [query], [row])
    far, own = lax.optimization_barrier((far, own))
    column = jnp.concatenate(far, 0)
    side = [send(column, 0, 1, 0), send(column, 0, -1, 0), send(column, 0, 2, 0)]
    both = [theirs, query]
    other = visit(join_kernel, "join_visit", valid_length, [theirs], [row, column])
    up2, down2 = send(up, 0, 0, 1), send(down, 0, 0, -1)
    state = visit(
        both_kernel, "both_visit", valid_length, both, [up, down], (*other, *own), STATE + STATE
    )
    other = visit(one_kernel, "side_visit", valid_length, [theirs], side, state[:2])
    late = [up2, down2]
    packet = jax.ShapeDtypeStruct((QROWS, ROWS), bf16)
    parcel = visit(
        parcel_kernel, "parcel_visit", valid_length, [theirs], late, other, STATE + (packet,)
    )[2]
    back = send(parcel, 1, 0, 0)
    own, own_max = visit(one_kernel, "own_visit", valid_length, [query], [column] + side + late, state[2:])
    return pl.pallas_call(
        merge_kernel,
        out_shape=(
            jax.ShapeDtypeStruct((2 * SPAN, ROWS), bf16),
            jax.ShapeDtypeStruct((HEADS, 2 * SPAN), f32),
        ),
        in_specs=[SMEM, VMEM, VMEM, VMEM],
        out_specs=(VMEM, VMEM),
        compiler_params=PARAMS,
        name="merge",
    )(positions, own, own_max, back)


def solution(mesh):
    placed = (
        P(("dp", "ctx"), None),
        P(("dp", "ctx"), None),
        P(("dp", "ctx"), None),
        P(("dp", "ctx")),
        P("dp"),
    )
    return jax.shard_map(
        shards,
        mesh=mesh,
        in_specs=placed,
        out_specs=(P(("dp", "ctx"), None), P(None, ("dp", "ctx"))),
        check_vma=False,
    )
```

time: 98.4 us -> 78.6 us (0.80)
  the two profiles are of different devices: /device:TPU:36 before, /device:TPU:4 now
where the time goes in v2:
time: 78.6 us; the launch traced here: 78.8 us
  Pallas kernels  40.4 us (51%)
  starting transfers between devices  29.7 us (38%)
  waiting for transfers between devices  6.22 us (8%)
  between operations  1.43 us (2%)
  other arithmetic  0.94 us (1%)
    pallas_call x6, Pallas kernels, visit(): pl.pallas_call(functools.partial(kernel, sizes), out_shape=shapes, in_spe...  35 us
    ppermute x15, starting transfers between devices, send(): return lax.ppermute(array, 'ctx', pairs)  29.7 us
    ppermute x15, waiting for transfers between devices, send(): return lax.ppermute(array, 'ctx', pairs)  6.22 us
    pallas_call x1, Pallas kernels, shards(): pl.pallas_call(pack_q_kernel, out_shape=(pltpu.VMEM((QROWS, ROWS), bf16),...  2.13 us
    pallas_call x1, Pallas kernels, shards(): pl.pallas_call(merge_kernel, out_shape=(jax.ShapeDtypeStruct((2 * SPAN, R...  1.7 us
    pallas_call x1, Pallas kernels, shards(): pl.pallas_call(pack_kv_kernel, out_shape=jax.ShapeDtypeStruct((BLOCK, DEP...  1.62 us
  transfers between devices with their start and end apart: 15, of which 3 were waited for; matrix products, arithmetic and copies ran while one was open for 1% of the time, Pallas kernels for 42%

profile of v2, /device:TPU:4, one launch (start us, length us, event | category | flops | bytes accessed | tf_op | source)
XLA Modules:
  0.0 78.8 jit_solution(3456480323777518920)
XLA Ops:
  0.6 1.6 %pack_kv.1 = bf16[528,128]{1,0:T(8,128)(2,1)} custom-call(s32[256]{0:T(256)} %pos_ref.5, bf16[256,128]{1,0:T(8,128)(2,1)} %k_ref.1, bf16[256,128]{1,0:T(8,128)(2,1)} %v_ref.1), custom_call_target="tpu_custom_call" | custom-call | tf_op jit(solution)/shard_map/pack_kv/pallas_call | solution.py:333
  2.2 1.2 %collective-permute-start.3 = (bf16[528,128]{1,0:T(8,128)(2,1)}, bf16[528,128]{1,0:T(8,128)(2,1)S(1)}, u32[]{:S(2)}, u32[]{:S(2)}) collective-permute-start(bf16[528,128]{1,0:T(8,128)(2,1)} %pack_kv.1), channel_id=1, source_target_pairs={{0,8},{1,9},{2,10},{3,11},{4,12},{5,13},{6,14},{7,15},{8,16},{9,17... | collective-permute-start | bytes 405512 | tf_op jit(solution)/shard_map/ppermute | solution.py:329
  3.4 0.8 %collective-permute-start.4 = (bf16[528,128]{1,0:T(8,128)(2,1)}, bf16[528,128]{1,0:T(8,128)(2,1)S(1)}, u32[]{:S(2)}, u32[]{:S(2)}) collective-permute-start(bf16[528,128]{1,0:T(8,128)(2,1)} %pack_kv.1), channel_id=1, source_target_pairs={{0,24},{1,25},{2,26},{3,27},{4,28},{5,29},{6,30},{7,31},{8,0},{9,1... | collective-permute-start | bytes 405512 | tf_op jit(solution)/shard_map/ppermute | solution.py:329
  4.3 3.5 %collective-permute-start.5 = (bf16[528,128]{1,0:T(8,128)(2,1)}, bf16[528,128]{1,0:T(8,128)(2,1)S(1)}, u32[]{:S(2)}, u32[]{:S(2)}) collective-permute-start(bf16[528,128]{1,0:T(8,128)(2,1)} %pack_kv.1), channel_id=1, source_target_pairs={{0,16},{1,17},{2,18},{3,19},{4,20},{5,21},{6,22},{7,23},{8,24},{9,... | collective-permute-start | bytes 405512 | tf_op jit(solution)/shard_map/ppermute | solution.py:329
  7.7 5.5 %collective-permute-start = (bf16[528,128]{1,0:T(8,128)(2,1)}, bf16[528,128]{1,0:T(8,128)(2,1)S(1)}, u32[]{:S(2)}, u32[]{:S(2)}) collective-permute-start(bf16[528,128]{1,0:T(8,128)(2,1)} %pack_kv.1), channel_id=1, source_target_pairs={{0,4},{1,5},{2,6},{3,7},{4,0},{5,1},{6,2},{7,3},{8,12},{9,13},{10,... | collective-permute-start | bytes 405512 | tf_op jit(solution)/shard_map/ppermute | solution.py:329
  13.2 1.9 %collective-permute-start.1 = (bf16[528,128]{1,0:T(8,128)(2,1)}, bf16[528,128]{1,0:T(8,128)(2,1)S(1)}, u32[]{:S(2)}, u32[]{:S(2)}) collective-permute-start(bf16[528,128]{1,0:T(8,128)(2,1)} %pack_kv.1), channel_id=1, source_target_pairs={{0,3},{1,4},{2,5},{3,6},{4,7},{5,0},{6,1},{7,2},{8,11},{9,12},{10,... | collective-permute-start | bytes 405512 | tf_op jit(solution)/shard_map/ppermute | solution.py:329
  15.8 2.1 %pack_q.1 = (bf16[272,1024]{1,0:T(8,128)(2,1)S(1)}, bf16[272,1024]{1,0:T(8,128)(2,1)}) custom-call(s32[256]{0:T(256)} %pos_ref.5, bf16[256,1024]{1,0:T(8,128)(2,1)} %q_ref.1), custom_call_target="tpu_custom_call" | custom-call | tf_op jit(solution)/shard_map/pack_q/pallas_call | solution.py:340
  17.9 0.0 collective-permute-done.3
  17.9 3.1 %collective-permute-start.2 = (bf16[528,128]{1,0:T(8,128)(2,1)}, bf16[528,128]{1,0:T(8,128)(2,1)S(1)}, u32[]{:S(2)}, u32[]{:S(2)}) collective-permute-start(bf16[528,128]{1,0:T(8,128)(2,1)} %pack_kv.1), channel_id=1, source_target_pairs={{0,5},{1,6},{2,7},{3,0},{4,1},{5,2},{6,3},{7,4},{8,13},{9,14},{10,... | collective-permute-start | bytes 405512 | tf_op jit(solution)/shard_map/ppermute | solution.py:329
  21.0 0.0 collective-permute-done.4
  21.0 1.6 %collective-permute-start.13 = (bf16[272,1024]{1,0:T(8,128)(2,1)}, bf16[272,1024]{1,0:T(8,128)(2,1)S(1)}, u32[]{:S(2)}, u32[]{:S(2)}) collective-permute-start(bf16[272,1024]{1,0:T(8,128)(2,1)} %get-tuple-element.28), channel_id=1, source_target_pairs={{0,32},{1,33},{2,34},{3,35},{4,36},{5,37},{6,38},{7,39},{8,40},{9,... | collective-permute-start | bytes 1671176 | tf_op jit(solution)/shard_map/ppermute | solution.py:329
  22.6 0.0 collective-permute-done.5
  22.6 0.9 %pad_maximum_fusion.kv.refs_0_ = bf16[2112,128]{1,0:T(8,128)(2,1)S(1)} fusion(bf16[528,128]{1,0:T(8,128)(2,1)S(1)} %collective-permute-done.5, bf16[528,128]{1,0:T(8,128)(2,1)S(1)} %collective-permute-done.4, bf16[528,128]{1,0:T(8,128)(2,1)S(1)} %collective-permute-done.3, bf16[528,128]{1,0:T(8,128)(2,1)} %pack_kv.1), kind=kLoop, calls=%fused_computation | loop fusion | flops 2162688 | bytes 1081344 | tf_op jit(solution)/shard_map/concatenate | solution.py:352
  23.5 0.1 collective-permute-start.11
  23.6 3.4 %first_visit.1 = (f32[2,144,1024]{2,1,0:T(8,128)S(1)}, f32[2,1,1024]{2,1,0:T(1,128)S(1)}) custom-call(s32[1]{0:T(128)S(6)} %copy.29.len_ref, bf16[272,1024]{1,0:T(8,128)(2,1)S(1)} %get-tuple-element.22.q_ref, bf16[2112,128]{1,0:T(8,128)(2,1)S(1)} %pad_maximum_fusion.kv.refs_0_), custom_call_target="tpu_custom_call" | custom-call | flops 2684354560 | bytes 540672 | tf_op jit(solution)/shard_map/first_visit/pallas_call | solution.py:305
  27.0 0.0 collective-permute-done
  27.0 2.1 %collective-permute-start.9 = (bf16[2112,128]{1,0:T(8,128)(2,1)S(1)}, bf16[2112,128]{1,0:T(8,128)(2,1)S(1)}, u32[]{:S(2)}, u32[]{:S(2)}) collective-permute-start(bf16[2112,128]{1,0:T(8,128)(2,1)S(1)} %pad_maximum_fusion.kv.refs_0_), channel_id=1, source_target_pairs={{0,1},{1,2},{2,3},{3,4},{4,5},{5,6},{6,7},{7,0},{8,9},{9,10},{10,1... | collective-permute-start | bytes 1622024 | tf_op jit(solution)/shard_map/ppermute | solution.py:329
  29.1 0.0 collective-permute-done.1
  29.1 0.5 collective-permute-done.2
  29.6 1.0 %collective-permute-start.6 = (bf16[1584,128]{1,0:T(8,128)(2,1)S(1)}, bf16[1584,128]{1,0:T(8,128)(2,1)S(1)}, u32[]{:S(2)}, u32[]{:S(2)}) collective-permute-start(bf16[1584,128]{1,0:T(8,128)(2,1)S(1)} %constant_dynamic-update-slice_fusion.refs_1_.refs_0_), channel_id=1, source_target_pairs={{0,8},{1,9},{2,10},{3,11},{4,12},{5,13},{6,14},{7,15},{8,16},{9,17... | collective-permute-start | bytes 1216520 | tf_op jit(solution)/shard_map/ppermute | solution.py:329
  30.6 1.1 %collective-permute-start.7 = (bf16[1584,128]{1,0:T(8,128)(2,1)S(1)}, bf16[1584,128]{1,0:T(8,128)(2,1)S(1)}, u32[]{:S(2)}, u32[]{:S(2)}) collective-permute-start(bf16[1584,128]{1,0:T(8,128)(2,1)S(1)} %constant_dynamic-update-slice_fusion.refs_1_.refs_0_), channel_id=1, source_target_pairs={{0,24},{1,25},{2,26},{3,27},{4,28},{5,29},{6,30},{7,31},{8,0},{9,1... | collective-permute-start | bytes 1216520 | tf_op jit(solution)/shard_map/ppermute | solution.py:329
  31.8 2.1 %collective-permute-done.13.q_ref.theirs_ref = bf16[272,1024]{1,0:T(8,128)(2,1)S(1)} collective-permute-done((bf16[272,1024]{1,0:T(8,128)(2,1)}, bf16[272,1024]{1,0:T(8,128)(2,1)S(1)}, u32[]{:S(2)}, u32[]{:S(2)}) %collective-permute-start.13) | collective-permute-done | bytes 557088 | tf_op jit(solution)/shard_map/ppermute | solution.py:329
  33.9 1.8 %collective-permute-start.8 = (bf16[1584,128]{1,0:T(8,128)(2,1)S(1)}, bf16[1584,128]{1,0:T(8,128)(2,1)S(1)}, u32[]{:S(2)}, u32[]{:S(2)}) collective-permute-start(bf16[1584,128]{1,0:T(8,128)(2,1)S(1)} %constant_dynamic-update-slice_fusion.refs_1_.refs_0_), channel_id=1, source_target_pairs={{0,16},{1,17},{2,18},{3,19},{4,20},{5,21},{6,22},{7,23},{8,24},{9,... | collective-permute-start | bytes 1216520 | tf_op jit(solution)/shard_map/ppermute | solution.py:329
  35.7 3.8 %join_visit.1 = (f32[2,144,1024]{2,1,0:T(8,128)S(1)}, f32[2,1,1024]{2,1,0:T(1,128)S(1)}) custom-call(s32[1]{0:T(128)S(6)} %copy.29.len_ref, bf16[272,1024]{1,0:T(8,128)(2,1)S(1)} %collective-permute-done.13.q_ref.theirs_ref, bf16[2112,128]{1,0:T(8,128)(2,1)S(1)} %pad_maximum_fusion.kv.refs_0_, ...), custom_call_target="tpu_custom_call" | custom-call | flops 4697620480 | bytes 946176 | tf_op jit(solution)/shard_map/join_visit/pallas_call | solution.py:305
  39.5 0.0 collective-permute-done.9.refs_0_
  39.5 2.1 %collective-permute-start.10 = (bf16[2112,128]{1,0:T(8,128)(2,1)S(1)}, bf16[2112,128]{1,0:T(8,128)(2,1)S(1)}, u32[]{:S(2)}, u32[]{:S(2)}) collective-permute-start(bf16[2112,128]{1,0:T(8,128)(2,1)S(1)} %collective-permute-done.9.refs_0_), channel_id=1, source_target_pairs={{0,1},{1,2},{2,3},{3,4},{4,5},{5,6},{6,7},{7,0},{8,9},{9,10},{10,1... | collective-permute-start | bytes 1622024 | tf_op jit(solution)/shard_map/ppermute | solution.py:329
  41.6 0.0 collective-permute-done.11.refs_1_
  41.6 2.3 %collective-permute-start.12 = (bf16[2112,128]{1,0:T(8,128)(2,1)S(1)}, bf16[2112,128]{1,0:T(8,128)(2,1)S(1)}, u32[]{:S(2)}, u32[]{:S(2)}) collective-permute-start(bf16[2112,128]{1,0:T(8,128)(2,1)S(1)} %collective-permute-done.11.refs_1_), channel_id=1, source_target_pairs={{0,7},{1,0},{2,1},{3,2},{4,3},{5,4},{6,5},{7,6},{8,15},{9,8},{10,9... | collective-permute-start | bytes 1622024 | tf_op jit(solution)/shard_map/ppermute | solution.py:329
  43.9 8.8 %both_visit.1 = (f32[2,144,1024]{2,1,0:T(8,128)S(1)}, f32[2,1,1024]{2,1,0:T(1,128)S(1)}, f32[2,144,1024]{2,1,0:T(8,128)S(1)}, f32[2,1,1024]{2,1,0:T(1,128)S(1)}) custom-call(s32[1]{0:T(128)S(6)} %copy.29.len_ref, ...), custom_call_target="tpu_custom_call", output_to_operand_aliasing={{0}: (5, {}), {1}: (6, {}), {2}: (7, {}), {3}: (8, {})} | custom-call | flops 10737418240 | bytes 1081344 | tf_op jit(solution)/shard_map/both_visit/pallas_call | solution.py:305
  52.7 0.0 collective-permute-done.6.refs_1_.refs_0_
  52.7 0.0 collective-permute-done.7.refs_2_.refs_1_
  52.7 0.0 collective-permute-done.8.refs_3_.refs_2_
  52.7 5.0 %side_visit.1 = (f32[2,144,1024]{2,1,0:T(8,128)S(1)}, f32[2,1,1024]{2,1,0:T(1,128)S(1)}) custom-call(s32[1]{0:T(128)S(6)} %copy.29.len_ref, bf16[272,1024]{1,0:T(8,128)(2,1)S(1)} %collective-permute-done.13.q_ref.theirs_ref, bf16[1584,128]{1,0:T(8,128)(2,1)S(1)} %collective-permute-done.6.refs_1_.refs_0_, ...), custom_call_target="tpu_custom_call", output_to_operand_aliasing={{0}: (5, {}), {1}: (6, {})} | custom-call | flops 6039797760 | bytes 1216512 | tf_op jit(solution)/shard_map/side_visit/pallas_call | solution.py:305
  57.7 0.0 collective-permute-done.10.refs_4_.refs_0_
  57.7 0.0 collective-permute-done.12.refs_5_.refs_1_
  57.7 4.1 %parcel_visit.1 = (f32[2,144,1024]{2,1,0:T(8,128)S(1)}, f32[2,1,1024]{2,1,0:T(1,128)S(1)}, bf16[272,1024]{1,0:T(8,128)(2,1)S(1)}) custom-call(s32[1]{0:T(128)S(6)} %copy.29.len_ref, bf16[272,1024]{1,0:T(8,128)(2,1)S(1)} %collective-permute-done.13.q_ref.theirs_ref, ...), custom_call_target="tpu_custom_call", output_to_operand_aliasing={{0}: (4, {}), {1}: (5, {})} | custom-call | flops 5368709120 | bytes 1081344 | tf_op jit(solution)/shard_map/parcel_visit/pallas_call | solution.py:305
  61.9 1.7 %collective-permute-start.14 = (bf16[272,1024]{1,0:T(8,128)(2,1)S(1)}, bf16[272,1024]{1,0:T(8,128)(2,1)S(1)}, u32[]{:S(2)}, u32[]{:S(2)}) collective-permute-start(bf16[272,1024]{1,0:T(8,128)(2,1)S(1)} %get-tuple-element.41), channel_id=1, source_target_pairs={{0,32},{1,33},{2,34},{3,35},{4,36},{5,37},{6,38},{7,39},{8,40},{9,... | collective-permute-start | bytes 1671176 | tf_op jit(solution)/shard_map/ppermute | solution.py:329
  63.6 0.0 copy-start
  63.6 9.9 %own_visit.1 = (f32[2,144,1024]{2,1,0:T(8,128)S(1)}, f32[2,1,1024]{2,1,0:T(1,128)S(1)}) custom-call(s32[1]{0:T(128)S(6)} %copy.29.len_ref, bf16[272,1024]{1,0:T(8,128)(2,1)S(1)} %get-tuple-element.22.q_ref, bf16[1584,128]{1,0:T(8,128)(2,1)S(1)} %constant_dynamic-update-slice_fusion.refs_1_.refs_0_, ...), custom_call_target="tpu_custom_call", output_to_operand_aliasing={{0}: (8, {}), {1}: (9, {})} | custom-call | flops 13421772800 | bytes 2703360 | tf_op jit(solution)/shard_map/own_visit/pallas_call | solution.py:305
  73.5 3.5 %collective-permute-done.14.theirs_ref = bf16[272,1024]{1,0:T(8,128)(2,1)S(1)} collective-permute-done((bf16[272,1024]{1,0:T(8,128)(2,1)S(1)}, bf16[272,1024]{1,0:T(8,128)(2,1)S(1)}, u32[]{:S(2)}, u32[]{:S(2)}) %collective-permute-start.14) | collective-permute-done | bytes 557088 | tf_op jit(solution)/shard_map/ppermute | solution.py:329
  77.1 0.0 copy-done
  77.1 1.7 %merge.1 = (bf16[256,1024]{1,0:T(8,128)(2,1)}, f32[8,256]{1,0:T(8,128)}) custom-call(s32[256]{0:T(256)S(1)} %copy-done, f32[2,144,1024]{2,1,0:T(8,128)S(1)} %get-tuple-element.35.o_ref, f32[2,1,1024]{2,1,0:T(1,128)S(1)} %get-tuple-element.36.m_ref, bf16[272,1024]{1,0:T(8,128)(2,1)S(1)} %collective-permute-done.14.theirs_ref), custom_call_target="tpu_custom_call" | custom-call | tf_op jit(solution)/shard_map/merge/pallas_call | solution.py:372
  (3 shorter events, 0.1 us)
Async XLA Ops:
  2.2 15.6 %collective-permute-start.3 = (bf16[528,128]{1,0:T(8,128)(2,1)}, bf16[528,128]{1,0:T(8,128)(2,1)S(1)}, u32[]{:S(2)}, u32[]{:S(2)}) collective-permute-start(bf16[528,128]{1,0:T(8,128)(2,1)} %pack_kv.1), channel_id=1, source_target_pairs={{0,8},{1,9},{2,10},{3,11},{4,12},{5,13},{6,14},{7,15},{8,16},{9,17... | collective-permute-start | bytes 405512 | tf_op jit(solution)/shard_map/ppermute | solution.py:329
  3.4 17.6 %collective-permute-start.4 = (bf16[528,128]{1,0:T(8,128)(2,1)}, bf16[528,128]{1,0:T(8,128)(2,1)S(1)}, u32[]{:S(2)}, u32[]{:S(2)}) collective-permute-start(bf16[528,128]{1,0:T(8,128)(2,1)} %pack_kv.1), channel_id=1, source_target_pairs={{0,24},{1,25},{2,26},{3,27},{4,28},{5,29},{6,30},{7,31},{8,0},{9,1... | collective-permute-start | bytes 405512 | tf_op jit(solution)/shard_map/ppermute | solution.py:329
  4.3 18.3 %collective-permute-start.5 = (bf16[528,128]{1,0:T(8,128)(2,1)}, bf16[528,128]{1,0:T(8,128)(2,1)S(1)}, u32[]{:S(2)}, u32[]{:S(2)}) collective-permute-start(bf16[528,128]{1,0:T(8,128)(2,1)} %pack_kv.1), channel_id=1, source_target_pairs={{0,16},{1,17},{2,18},{3,19},{4,20},{5,21},{6,22},{7,23},{8,24},{9,... | collective-permute-start | bytes 405512 | tf_op jit(solution)/shard_map/ppermute | solution.py:329
  7.7 19.3 %collective-permute-start = (bf16[528,128]{1,0:T(8,128)(2,1)}, bf16[528,128]{1,0:T(8,128)(2,1)S(1)}, u32[]{:S(2)}, u32[]{:S(2)}) collective-permute-start(bf16[528,128]{1,0:T(8,128)(2,1)} %pack_kv.1), channel_id=1, source_target_pairs={{0,4},{1,5},{2,6},{3,7},{4,0},{5,1},{6,2},{7,3},{8,12},{9,13},{10,... | collective-permute-start | bytes 405512 | tf_op jit(solution)/shard_map/ppermute | solution.py:329
  13.2 15.9 %collective-permute-start.1 = (bf16[528,128]{1,0:T(8,128)(2,1)}, bf16[528,128]{1,0:T(8,128)(2,1)S(1)}, u32[]{:S(2)}, u32[]{:S(2)}) collective-permute-start(bf16[528,128]{1,0:T(8,128)(2,1)} %pack_kv.1), channel_id=1, source_target_pairs={{0,3},{1,4},{2,5},{3,6},{4,7},{5,0},{6,1},{7,2},{8,11},{9,12},{10,... | collective-permute-start | bytes 405512 | tf_op jit(solution)/shard_map/ppermute | solution.py:329
  17.9 11.7 %collective-permute-start.2 = (bf16[528,128]{1,0:T(8,128)(2,1)}, bf16[528,128]{1,0:T(8,128)(2,1)S(1)}, u32[]{:S(2)}, u32[]{:S(2)}) collective-permute-start(bf16[528,128]{1,0:T(8,128)(2,1)} %pack_kv.1), channel_id=1, source_target_pairs={{0,5},{1,6},{2,7},{3,0},{4,1},{5,2},{6,3},{7,4},{8,13},{9,14},{10,... | collective-permute-start | bytes 405512 | tf_op jit(solution)/shard_map/ppermute | solution.py:329
  21.0 12.9 %collective-permute-start.13 = (bf16[272,1024]{1,0:T(8,128)(2,1)}, bf16[272,1024]{1,0:T(8,128)(2,1)S(1)}, u32[]{:S(2)}, u32[]{:S(2)}) collective-permute-start(bf16[272,1024]{1,0:T(8,128)(2,1)} %get-tuple-element.28), channel_id=1, source_target_pairs={{0,32},{1,33},{2,34},{3,35},{4,36},{5,37},{6,38},{7,39},{8,40},{9,... | collective-permute-start | bytes 1671176 | tf_op jit(solution)/shard_map/ppermute | solution.py:329
  23.5 18.1 %collective-permute-start.11 = (bf16[2112,128]{1,0:T(8,128)(2,1)S(1)}, bf16[2112,128]{1,0:T(8,128)(2,1)S(1)}, u32[]{:S(2)}, u32[]{:S(2)}) collective-permute-start(bf16[2112,128]{1,0:T(8,128)(2,1)S(1)} %pad_maximum_fusion.kv.refs_0_), channel_id=1, source_target_pairs={{0,7},{1,0},{2,1},{3,2},{4,3},{5,4},{6,5},{7,6},{8,15},{9,8},{10,9... | collective-permute-start | bytes 1622024 | tf_op jit(solution)/shard_map/ppermute | solution.py:329
  27.0 12.5 %collective-permute-start.9 = (bf16[2112,128]{1,0:T(8,128)(2,1)S(1)}, bf16[2112,128]{1,0:T(8,128)(2,1)S(1)}, u32[]{:S(2)}, u32[]{:S(2)}) collective-permute-start(bf16[2112,128]{1,0:T(8,128)(2,1)S(1)} %pad_maximum_fusion.kv.refs_0_), channel_id=1, source_target_pairs={{0,1},{1,2},{2,3},{3,4},{4,5},{5,6},{6,7},{7,0},{8,9},{9,10},{10,1... | collective-permute-start | bytes 1622024 | tf_op jit(solution)/shard_map/ppermute | solution.py:329
  29.6 23.0 %collective-permute-start.6 = (bf16[1584,128]{1,0:T(8,128)(2,1)S(1)}, bf16[1584,128]{1,0:T(8,128)(2,1)S(1)}, u32[]{:S(2)}, u32[]{:S(2)}) collective-permute-start(bf16[1584,128]{1,0:T(8,128)(2,1)S(1)} %constant_dynamic-update-slice_fusion.refs_1_.refs_0_), channel_id=1, source_target_pairs={{0,8},{1,9},{2,10},{3,11},{4,12},{5,13},{6,14},{7,15},{8,16},{9,17... | collective-permute-start | bytes 1216520 | tf_op jit(solution)/shard_map/ppermute | solution.py:329
  30.6 22.1 %collective-permute-start.7 = (bf16[1584,128]{1,0:T(8,128)(2,1)S(1)}, bf16[1584,128]{1,0:T(8,128)(2,1)S(1)}, u32[]{:S(2)}, u32[]{:S(2)}) collective-permute-start(bf16[1584,128]{1,0:T(8,128)(2,1)S(1)} %constant_dynamic-update-slice_fusion.refs_1_.refs_0_), channel_id=1, source_target_pairs={{0,24},{1,25},{2,26},{3,27},{4,28},{5,29},{6,30},{7,31},{8,0},{9,1... | collective-permute-start | bytes 1216520 | tf_op jit(solution)/shard_map/ppermute | solution.py:329
  33.9 18.8 %collective-permute-start.8 = (bf16[1584,128]{1,0:T(8,128)(2,1)S(1)}, bf16[1584,128]{1,0:T(8,128)(2,1)S(1)}, u32[]{:S(2)}, u32[]{:S(2)}) collective-permute-start(bf16[1584,128]{1,0:T(8,128)(2,1)S(1)} %constant_dynamic-update-slice_fusion.refs_1_.refs_0_), channel_id=1, source_target_pairs={{0,16},{1,17},{2,18},{3,19},{4,20},{5,21},{6,22},{7,23},{8,24},{9,... | collective-permute-start | bytes 1216520 | tf_op jit(solution)/shard_map/ppermute | solution.py:329
  39.5 18.2 %collective-permute-start.10 = (bf16[2112,128]{1,0:T(8,128)(2,1)S(1)}, bf16[2112,128]{1,0:T(8,128)(2,1)S(1)}, u32[]{:S(2)}, u32[]{:S(2)}) collective-permute-start(bf16[2112,128]{1,0:T(8,128)(2,1)S(1)} %collective-permute-done.9.refs_0_), channel_id=1, source_target_pairs={{0,1},{1,2},{2,3},{3,4},{4,5},{5,6},{6,7},{7,0},{8,9},{9,10},{10,1... | collective-permute-start | bytes 1622024 | tf_op jit(solution)/shard_map/ppermute | solution.py:329
  41.6 16.1 %collective-permute-start.12 = (bf16[2112,128]{1,0:T(8,128)(2,1)S(1)}, bf16[2112,128]{1,0:T(8,128)(2,1)S(1)}, u32[]{:S(2)}, u32[]{:S(2)}) collective-permute-start(bf16[2112,128]{1,0:T(8,128)(2,1)S(1)} %collective-permute-done.11.refs_1_), channel_id=1, source_target_pairs={{0,7},{1,0},{2,1},{3,2},{4,3},{5,4},{6,5},{7,6},{8,15},{9,8},{10,9... | collective-permute-start | bytes 1622024 | tf_op jit(solution)/shard_map/ppermute | solution.py:329
  61.9 15.2 %collective-permute-start.14 = (bf16[272,1024]{1,0:T(8,128)(2,1)S(1)}, bf16[272,1024]{1,0:T(8,128)(2,1)S(1)}, u32[]{:S(2)}, u32[]{:S(2)}) collective-permute-start(bf16[272,1024]{1,0:T(8,128)(2,1)S(1)} %get-tuple-element.41), channel_id=1, source_target_pairs={{0,32},{1,33},{2,34},{3,35},{4,36},{5,37},{6,38},{7,39},{8,40},{9,... | collective-permute-start | bytes 1671176 | tf_op jit(solution)/shard_map/ppermute | solution.py:329
  63.6 13.5 %copy-start = (s32[256]{0:T(256)S(1)}, s32[256]{0:T(256)}, u32[]{:S(2)}) copy-start(s32[256]{0:T(256)} %pos_ref.5) | copy-start | bytes 3076

commit v3 on v2

--- a/solution.py
+++ b/solution.py
@@ -65,7 +65,7 @@
     return jnp.max(tile.astype(f32)).astype(jnp.int32)
 
 
-def attend(sizes, kv_refs, kv, len_ref, q_ref, state, work, sems, fetch=True):
+def attend(sizes, kv_refs, kv, len_ref, q_ref, state, work, sems, fetch=True, since=0):
     o_ref, m_ref = state
     s_ref, addr, base, slot_of = work
     total = sum(sizes)
@@ -84,7 +84,7 @@
 
     length = len_ref[0]
     mine = run_of(q_ref[2 * SPAN : 2 * SPAN + 16, :DEPTH])
-    seen = range(total)
+    seen = range(since, total)
     runs = {b: run_of(kv[b * BLOCK + 4 * SPAN : (b + 1) * BLOCK, :]) for b in seen}
 
     def append(count, slot, row, first, wanted):
@@ -94,7 +94,7 @@
         return count + wanted.astype(jnp.int32)
 
     def pad(count, slot):
-        return append(count, slot, 0, SHUT, (count & 1) == 1)
+        return append(count, slot, since * BLOCK, SHUT, (count & 1) == 1)
 
     count = jnp.int32(0)
     for b in seen:
@@ -224,7 +224,7 @@
     n = len(sizes)
     _, _, _, _, o1, m1, o2, m2, kv, sems, *work = refs[n:]
     attend(sizes, refs[:n], kv, len_ref, theirs_ref, (o1, m1), work, sems)
-    attend(sizes, refs[:n], kv, len_ref, q_ref, (o2, m2), work, sems, False)
+    attend(sizes, refs[:n], kv, len_ref, q_ref, (o2, m2), work, sems, False, sizes[0])
 
 
 def one_kernel(sizes, len_ref, q_ref, *refs):
@@ -349,6 +349,7 @@
     far = [send(block, 0, 0, 4), send(block, 0, 0, 3), send(block, 0, 0, -3)]
     theirs = send(outgoing, 1, 0, 0)
 
+    near, far[0] = lax.optimization_barrier((near, far[0]))
     row = jnp.concatenate(near, 0)
     up, down = send(row, 0, 0, 1), send(row, 0, 0, -1)
     own = visit(first_kernel, "first_visit", valid_length, [query], [row])
@@ -368,7 +369,7 @@
         parcel_kernel, "parcel_visit", valid_length, [theirs], late, other, STATE + (packet,)
     )[2]
     back = send(parcel, 1, 0, 0)
-    own, own_max = visit(one_kernel, "own_visit", valid_length, [query], [column] + side + late, state[2:])
+    own, own_max = visit(one_kernel, "own_visit", valid_length, [query], [column, up] + side + late, state[2:])
     return pl.pallas_call(
         merge_kernel,
         out_shape=(

time: 78.6 us -> 78.6 us (level)
  the two profiles are of different devices: /device:TPU:4 before, /device:TPU:8 now
where the time goes in v3:
time: 78.6 us; the launch traced here: 78.7 us
  Pallas kernels  45.1 us (57%)
  starting transfers between devices  28.3 us (36%)
  waiting for transfers between devices  2.85 us (4%)
  between operations  1.5 us (2%)
  local copies, waits for them, and re-layouts  1.03 us (1%)
    pallas_call x6, Pallas kernels, visit(): pl.pallas_call(functools.partial(kernel, sizes), out_shape=shapes, in_spe...  39.6 us
    ppermute x15, starting transfers between devices, send(): return lax.ppermute(array, 'ctx', pairs)  28.3 us
    ppermute x15, waiting for transfers between devices, send(): return lax.ppermute(array, 'ctx', pairs)  2.85 us
    pallas_call x1, Pallas kernels, shards(): pl.pallas_call(pack_q_kernel, out_shape=(pltpu.VMEM((QROWS, ROWS), bf16),...  2.13 us
    pallas_call x1, Pallas kernels, shards(): pl.pallas_call(merge_kernel, out_shape=(jax.ShapeDtypeStruct((2 * SPAN, R...  1.69 us
    pallas_call x1, Pallas kernels, shards(): pl.pallas_call(pack_kv_kernel, out_shape=jax.ShapeDtypeStruct((BLOCK, DEP...  1.62 us
  transfers between devices with their start and end apart: 15, of which 1 were waited for; matrix products, arithmetic and copies ran while one was open for 1% of the time, Pallas kernels for 47%

profile of v3, /device:TPU:8, one launch (start us, length us, event | category | flops | bytes accessed | tf_op | source)
XLA Modules:
  0.0 78.7 jit_solution(15386242005184576036)
XLA Ops:
  0.6 1.6 %pack_kv.1 = bf16[528,128]{1,0:T(8,128)(2,1)} custom-call(s32[256]{0:T(256)} %pos_ref.5, bf16[256,128]{1,0:T(8,128)(2,1)} %k_ref.1, bf16[256,128]{1,0:T(8,128)(2,1)} %v_ref.1), custom_call_target="tpu_custom_call" | custom-call | tf_op jit(solution)/shard_map/pack_kv/pallas_call | solution.py:333
  2.2 1.5 %collective-permute-start = (bf16[528,128]{1,0:T(8,128)(2,1)}, bf16[528,128]{1,0:T(8,128)(2,1)S(1)}, u32[]{:S(2)}, u32[]{:S(2)}) collective-permute-start(bf16[528,128]{1,0:T(8,128)(2,1)} %pack_kv.1), channel_id=1, source_target_pairs={{0,8},{1,9},{2,10},{3,11},{4,12},{5,13},{6,14},{7,15},{8,16},{9,17... | collective-permute-start | bytes 405512 | tf_op jit(solution)/shard_map/ppermute | solution.py:329
  3.7 1.7 %collective-permute-start.1 = (bf16[528,128]{1,0:T(8,128)(2,1)}, bf16[528,128]{1,0:T(8,128)(2,1)S(1)}, u32[]{:S(2)}, u32[]{:S(2)}) collective-permute-start(bf16[528,128]{1,0:T(8,128)(2,1)} %pack_kv.1), channel_id=1, source_target_pairs={{0,24},{1,25},{2,26},{3,27},{4,28},{5,29},{6,30},{7,31},{8,0},{9,1... | collective-permute-start | bytes 405512 | tf_op jit(solution)/shard_map/ppermute | solution.py:329
  5.5 1.8 %collective-permute-start.2 = (bf16[528,128]{1,0:T(8,128)(2,1)}, bf16[528,128]{1,0:T(8,128)(2,1)S(1)}, u32[]{:S(2)}, u32[]{:S(2)}) collective-permute-start(bf16[528,128]{1,0:T(8,128)(2,1)} %pack_kv.1), channel_id=1, source_target_pairs={{0,16},{1,17},{2,18},{3,19},{4,20},{5,21},{6,22},{7,23},{8,24},{9,... | collective-permute-start | bytes 405512 | tf_op jit(solution)/shard_map/ppermute | solution.py:329
  7.3 7.2 %collective-permute-start.3 = (bf16[528,128]{1,0:T(8,128)(2,1)}, bf16[528,128]{1,0:T(8,128)(2,1)S(1)}, u32[]{:S(2)}, u32[]{:S(2)}) collective-permute-start(bf16[528,128]{1,0:T(8,128)(2,1)} %pack_kv.1), channel_id=1, source_target_pairs={{0,4},{1,5},{2,6},{3,7},{4,0},{5,1},{6,2},{7,3},{8,12},{9,13},{10,... | collective-permute-start | bytes 405512 | tf_op jit(solution)/shard_map/ppermute | solution.py:329
  14.5 1.9 %collective-permute-start.4 = (bf16[528,128]{1,0:T(8,128)(2,1)}, bf16[528,128]{1,0:T(8,128)(2,1)S(1)}, u32[]{:S(2)}, u32[]{:S(2)}) collective-permute-start(bf16[528,128]{1,0:T(8,128)(2,1)} %pack_kv.1), channel_id=1, source_target_pairs={{0,3},{1,4},{2,5},{3,6},{4,7},{5,0},{6,1},{7,2},{8,11},{9,12},{10,... | collective-permute-start | bytes 405512 | tf_op jit(solution)/shard_map/ppermute | solution.py:329
  17.1 2.1 %pack_q.1 = (bf16[272,1024]{1,0:T(8,128)(2,1)S(1)}, bf16[272,1024]{1,0:T(8,128)(2,1)}) custom-call(s32[256]{0:T(256)} %pos_ref.5, bf16[256,1024]{1,0:T(8,128)(2,1)} %q_ref.1), custom_call_target="tpu_custom_call" | custom-call | tf_op jit(solution)/shard_map/pack_q/pallas_call | solution.py:340
  19.2 0.0 collective-permute-done
  19.2 3.1 %collective-permute-start.5 = (bf16[528,128]{1,0:T(8,128)(2,1)}, bf16[528,128]{1,0:T(8,128)(2,1)S(1)}, u32[]{:S(2)}, u32[]{:S(2)}) collective-permute-start(bf16[528,128]{1,0:T(8,128)(2,1)} %pack_kv.1), channel_id=1, source_target_pairs={{0,5},{1,6},{2,7},{3,0},{4,1},{5,2},{6,3},{7,4},{8,13},{9,14},{10,... | collective-permute-start | bytes 405512 | tf_op jit(solution)/shard_map/ppermute | solution.py:329
  22.3 0.0 collective-permute-done.1
  22.3 0.5 collective-permute-start.13
  22.8 0.0 collective-permute-done.2
  22.8 2.8 %collective-permute-done.3 = bf16[528,128]{1,0:T(8,128)(2,1)S(1)} collective-permute-done((bf16[528,128]{1,0:T(8,128)(2,1)}, bf16[528,128]{1,0:T(8,128)(2,1)S(1)}, u32[]{:S(2)}, u32[]{:S(2)}) %collective-permute-start.3) | collective-permute-done | bytes 135200 | tf_op jit(solution)/shard_map/ppermute | solution.py:329
  25.6 0.9 %constant_dynamic-update-slice_fusion.3 = bf16[2112,128]{1,0:T(8,128)(2,1)S(1)} fusion(bf16[528,128]{1,0:T(8,128)(2,1)} %pack_kv.1), kind=kLoop, calls=%fused_computation.3 | loop fusion | bytes 270336
  26.6 0.1 collective-permute-start.11
  26.7 2.0 %collective-permute-start.6 = (bf16[2112,128]{1,0:T(8,128)(2,1)S(1)}, bf16[2112,128]{1,0:T(8,128)(2,1)S(1)}, u32[]{:S(2)}, u32[]{:S(2)}) collective-permute-start(bf16[2112,128]{1,0:T(8,128)(2,1)S(1)} %constant_dynamic-update-slice_fusion.kv.refs_0_), channel_id=1, source_target_pairs={{0,1},{1,2},{2,3},{3,4},{4,5},{5,6},{6,7},{7,0},{8,9},{9,10},{10,1... | collective-permute-start | bytes 1622024 | tf_op jit(solution)/shard_map/ppermute | solution.py:329
  28.7 3.4 %first_visit.1 = (f32[2,144,1024]{2,1,0:T(8,128)S(1)}, f32[2,1,1024]{2,1,0:T(1,128)S(1)}) custom-call(s32[1]{0:T(128)S(6)} %copy.32.len_ref, bf16[272,1024]{1,0:T(8,128)(2,1)S(1)} %get-tuple-element.27.q_ref, bf16[2112,128]{1,0:T(8,128)(2,1)S(1)} %constant_dynamic-update-slice_fusion.kv.refs_0_), custom_call_target="tpu_custom_call" | custom-call | flops 2684354560 | bytes 540672 | tf_op jit(solution)/shard_map/first_visit/pallas_call | solution.py:305
  32.0 0.0 collective-permute-done.4
  32.1 0.0 collective-permute-done.5
  32.1 0.1 collective-permute-start.7
  32.2 3.2 %collective-permute-start.8 = (bf16[1584,128]{1,0:T(8,128)(2,1)S(1)}, bf16[1584,128]{1,0:T(8,128)(2,1)S(1)}, u32[]{:S(2)}, u32[]{:S(2)}) collective-permute-start(bf16[1584,128]{1,0:T(8,128)(2,1)S(1)} %constant_dynamic-update-slice_fusion.4.refs_1_.refs_0_), channel_id=1, source_target_pairs={{0,24},{1,25},{2,26},{3,27},{4,28},{5,29},{6,30},{7,31},{8,0},{9,1... | collective-permute-start | bytes 1216520 | tf_op jit(solution)/shard_map/ppermute | solution.py:329
  35.5 0.0 collective-permute-done.13.q_ref.theirs_ref
  35.5 1.5 %collective-permute-start.9 = (bf16[1584,128]{1,0:T(8,128)(2,1)S(1)}, bf16[1584,128]{1,0:T(8,128)(2,1)S(1)}, u32[]{:S(2)}, u32[]{:S(2)}) collective-permute-start(bf16[1584,128]{1,0:T(8,128)(2,1)S(1)} %constant_dynamic-update-slice_fusion.4.refs_1_.refs_0_), channel_id=1, source_target_pairs={{0,16},{1,17},{2,18},{3,19},{4,20},{5,21},{6,22},{7,23},{8,24},{9,... | collective-permute-start | bytes 1216520 | tf_op jit(solution)/shard_map/ppermute | solution.py:329
  36.9 4.7 %join_visit.1 = (f32[2,144,1024]{2,1,0:T(8,128)S(1)}, f32[2,1,1024]{2,1,0:T(1,128)S(1)}) custom-call(s32[1]{0:T(128)S(6)} %copy.32.len_ref, bf16[272,1024]{1,0:T(8,128)(2,1)S(1)} %collective-permute-done.13.q_ref.theirs_ref, bf16[2112,128]{1,0:T(8,128)(2,1)S(1)} %constant_dynamic-update-slice_fusion.kv.refs_0_, ...), custom_call_target="tpu_custom_call" | custom-call | flops 4697620480 | bytes 946176 | tf_op jit(solution)/shard_map/join_visit/pallas_call | solution.py:305
  41.6 0.0 collective-permute-done.6.refs_0_.refs_1_
  41.6 1.1 %collective-permute-start.10 = (bf16[2112,128]{1,0:T(8,128)(2,1)S(1)}, bf16[2112,128]{1,0:T(8,128)(2,1)S(1)}, u32[]{:S(2)}, u32[]{:S(2)}) collective-permute-start(bf16[2112,128]{1,0:T(8,128)(2,1)S(1)} %collective-permute-done.6.refs_0_.refs_1_), channel_id=1, source_target_pairs={{0,1},{1,2},{2,3},{3,4},{4,5},{5,6},{6,7},{7,0},{8,9},{9,10},{10,1... | collective-permute-start | bytes 1622024 | tf_op jit(solution)/shard_map/ppermute | solution.py:329
  42.7 0.0 collective-permute-done.11.refs_1_
  42.7 2.3 %collective-permute-start.12 = (bf16[2112,128]{1,0:T(8,128)(2,1)S(1)}, bf16[2112,128]{1,0:T(8,128)(2,1)S(1)}, u32[]{:S(2)}, u32[]{:S(2)}) collective-permute-start(bf16[2112,128]{1,0:T(8,128)(2,1)S(1)} %collective-permute-done.11.refs_1_), channel_id=1, source_target_pairs={{0,7},{1,0},{2,1},{3,2},{4,3},{5,4},{6,5},{7,6},{8,15},{9,8},{10,9... | collective-permute-start | bytes 1622024 | tf_op jit(solution)/shard_map/ppermute | solution.py:329
  45.0 8.0 %both_visit.1 = (f32[2,144,1024]{2,1,0:T(8,128)S(1)}, f32[2,1,1024]{2,1,0:T(1,128)S(1)}, f32[2,144,1024]{2,1,0:T(8,128)S(1)}, f32[2,1,1024]{2,1,0:T(1,128)S(1)}) custom-call(s32[1]{0:T(128)S(6)} %copy.32.len_ref, ...), custom_call_target="tpu_custom_call", output_to_operand_aliasing={{0}: (5, {}), {1}: (6, {}), {2}: (7, {}), {3}: (8, {})} | custom-call | flops 10737418240 | bytes 1081344 | tf_op jit(solution)/shard_map/both_visit/pallas_call | solution.py:305
  53.0 0.0 collective-permute-done.7.refs_2_.refs_0_
  53.0 0.0 collective-permute-done.8.refs_3_.refs_1_
  53.1 0.0 collective-permute-done.9.refs_4_.refs_2_
  53.1 5.9 %side_visit.1 = (f32[2,144,1024]{2,1,0:T(8,128)S(1)}, f32[2,1,1024]{2,1,0:T(1,128)S(1)}) custom-call(s32[1]{0:T(128)S(6)} %copy.32.len_ref, bf16[272,1024]{1,0:T(8,128)(2,1)S(1)} %collective-permute-done.13.q_ref.theirs_ref, bf16[1584,128]{1,0:T(8,128)(2,1)S(1)} %collective-permute-done.7.refs_2_.refs_0_, ...), custom_call_target="tpu_custom_call", output_to_operand_aliasing={{0}: (5, {}), {1}: (6, {})} | custom-call | flops 6039797760 | bytes 1216512 | tf_op jit(solution)/shard_map/side_visit/pallas_call | solution.py:305
  58.9 0.0 collective-permute-done.10.refs_5_.refs_0_
  58.9 0.0 collective-permute-done.12.refs_6_.refs_1_
  58.9 5.0 %parcel_visit.1 = (f32[2,144,1024]{2,1,0:T(8,128)S(1)}, f32[2,1,1024]{2,1,0:T(1,128)S(1)}, bf16[272,1024]{1,0:T(8,128)(2,1)S(1)}) custom-call(s32[1]{0:T(128)S(6)} %copy.32.len_ref, bf16[272,1024]{1,0:T(8,128)(2,1)S(1)} %collective-permute-done.13.q_ref.theirs_ref, ...), custom_call_target="tpu_custom_call", output_to_operand_aliasing={{0}: (4, {}), {1}: (5, {})} | custom-call | flops 5368709120 | bytes 1081344 | tf_op jit(solution)/shard_map/parcel_visit/pallas_call | solution.py:305
  64.0 0.3 collective-permute-start.14
  64.3 0.0 copy-start
  64.3 12.7 %own_visit.1 = (f32[2,144,1024]{2,1,0:T(8,128)S(1)}, f32[2,1,1024]{2,1,0:T(1,128)S(1)}) custom-call(s32[1]{0:T(128)S(6)} %copy.32.len_ref, bf16[272,1024]{1,0:T(8,128)(2,1)S(1)} %get-tuple-element.27.q_ref, bf16[1584,128]{1,0:T(8,128)(2,1)S(1)} %constant_dynamic-update-slice_fusion.4.refs_1_.refs_0_, ...), custom_call_target="tpu_custom_call", output_to_operand_aliasing={{0}: (9, {}), {1}: (10, {})} | custom-call | flops 16106127360 | bytes 3244032 | tf_op jit(solution)/shard_map/own_visit/pallas_call | solution.py:305
  77.0 0.0 collective-permute-done.14.theirs_ref
  77.0 0.0 copy-done
  77.0 1.7 %merge.1 = (bf16[256,1024]{1,0:T(8,128)(2,1)}, f32[8,256]{1,0:T(8,128)}) custom-call(s32[256]{0:T(256)S(1)} %copy-done, f32[2,144,1024]{2,1,0:T(8,128)S(1)} %get-tuple-element.45.o_ref, f32[2,1,1024]{2,1,0:T(1,128)S(1)} %get-tuple-element.46.m_ref, bf16[272,1024]{1,0:T(8,128)(2,1)S(1)} %collective-permute-done.14.theirs_ref), custom_call_target="tpu_custom_call" | custom-call | tf_op jit(solution)/shard_map/merge/pallas_call | solution.py:373
  (6 shorter events, 0.1 us)
Async XLA Ops:
  2.2 16.9 %collective-permute-start = (bf16[528,128]{1,0:T(8,128)(2,1)}, bf16[528,128]{1,0:T(8,128)(2,1)S(1)}, u32[]{:S(2)}, u32[]{:S(2)}) collective-permute-start(bf16[528,128]{1,0:T(8,128)(2,1)} %pack_kv.1), channel_id=1, source_target_pairs={{0,8},{1,9},{2,10},{3,11},{4,12},{5,13},{6,14},{7,15},{8,16},{9,17... | collective-permute-start | bytes 405512 | tf_op jit(solution)/shard_map/ppermute | solution.py:329
  3.7 18.6 %collective-permute-start.1 = (bf16[528,128]{1,0:T(8,128)(2,1)}, bf16[528,128]{1,0:T(8,128)(2,1)S(1)}, u32[]{:S(2)}, u32[]{:S(2)}) collective-permute-start(bf16[528,128]{1,0:T(8,128)(2,1)} %pack_kv.1), channel_id=1, source_target_pairs={{0,24},{1,25},{2,26},{3,27},{4,28},{5,29},{6,30},{7,31},{8,0},{9,1... | collective-permute-start | bytes 405512 | tf_op jit(solution)/shard_map/ppermute | solution.py:329
  5.5 17.3 %collective-permute-start.2 = (bf16[528,128]{1,0:T(8,128)(2,1)}, bf16[528,128]{1,0:T(8,128)(2,1)S(1)}, u32[]{:S(2)}, u32[]{:S(2)}) collective-permute-start(bf16[528,128]{1,0:T(8,128)(2,1)} %pack_kv.1), channel_id=1, source_target_pairs={{0,16},{1,17},{2,18},{3,19},{4,20},{5,21},{6,22},{7,23},{8,24},{9,... | collective-permute-start | bytes 405512 | tf_op jit(solution)/shard_map/ppermute | solution.py:329
  7.3 18.3 %collective-permute-start.3 = (bf16[528,128]{1,0:T(8,128)(2,1)}, bf16[528,128]{1,0:T(8,128)(2,1)S(1)}, u32[]{:S(2)}, u32[]{:S(2)}) collective-permute-start(bf16[528,128]{1,0:T(8,128)(2,1)} %pack_kv.1), channel_id=1, source_target_pairs={{0,4},{1,5},{2,6},{3,7},{4,0},{5,1},{6,2},{7,3},{8,12},{9,13},{10,... | collective-permute-start | bytes 405512 | tf_op jit(solution)/shard_map/ppermute | solution.py:329
  14.5 17.6 %collective-permute-start.4 = (bf16[528,128]{1,0:T(8,128)(2,1)}, bf16[528,128]{1,0:T(8,128)(2,1)S(1)}, u32[]{:S(2)}, u32[]{:S(2)}) collective-permute-start(bf16[528,128]{1,0:T(8,128)(2,1)} %pack_kv.1), channel_id=1, source_target_pairs={{0,3},{1,4},{2,5},{3,6},{4,7},{5,0},{6,1},{7,2},{8,11},{9,12},{10,... | collective-permute-start | bytes 405512 | tf_op jit(solution)/shard_map/ppermute | solution.py:329
  19.2 12.9 %collective-permute-start.5 = (bf16[528,128]{1,0:T(8,128)(2,1)}, bf16[528,128]{1,0:T(8,128)(2,1)S(1)}, u32[]{:S(2)}, u32[]{:S(2)}) collective-permute-start(bf16[528,128]{1,0:T(8,128)(2,1)} %pack_kv.1), channel_id=1, source_target_pairs={{0,5},{1,6},{2,7},{3,0},{4,1},{5,2},{6,3},{7,4},{8,13},{9,14},{10,... | collective-permute-start | bytes 405512 | tf_op jit(solution)/shard_map/ppermute | solution.py:329
  22.3 13.2 %collective-permute-start.13 = (bf16[272,1024]{1,0:T(8,128)(2,1)}, bf16[272,1024]{1,0:T(8,128)(2,1)S(1)}, u32[]{:S(2)}, u32[]{:S(2)}) collective-permute-start(bf16[272,1024]{1,0:T(8,128)(2,1)} %get-tuple-element.38), channel_id=1, source_target_pairs={{0,32},{1,33},{2,34},{3,35},{4,36},{5,37},{6,38},{7,39},{8,40},{9,... | collective-permute-start | bytes 1671176 | tf_op jit(solution)/shard_map/ppermute | solution.py:329
  26.6 16.2 %collective-permute-start.11 = (bf16[2112,128]{1,0:T(8,128)(2,1)S(1)}, bf16[2112,128]{1,0:T(8,128)(2,1)S(1)}, u32[]{:S(2)}, u32[]{:S(2)}) collective-permute-start(bf16[2112,128]{1,0:T(8,128)(2,1)S(1)} %constant_dynamic-update-slice_fusion.kv.refs_0_), channel_id=1, source_target_pairs={{0,7},{1,0},{2,1},{3,2},{4,3},{5,4},{6,5},{7,6},{8,15},{9,8},{10,9... | collective-permute-start | bytes 1622024 | tf_op jit(solution)/shard_map/ppermute | solution.py:329
  26.7 15.0 %collective-permute-start.6 = (bf16[2112,128]{1,0:T(8,128)(2,1)S(1)}, bf16[2112,128]{1,0:T(8,128)(2,1)S(1)}, u32[]{:S(2)}, u32[]{:S(2)}) collective-permute-start(bf16[2112,128]{1,0:T(8,128)(2,1)S(1)} %constant_dynamic-update-slice_fusion.kv.refs_0_), channel_id=1, source_target_pairs={{0,1},{1,2},{2,3},{3,4},{4,5},{5,6},{6,7},{7,0},{8,9},{9,10},{10,1... | collective-permute-start | bytes 1622024 | tf_op jit(solution)/shard_map/ppermute | solution.py:329
  32.1 20.9 %collective-permute-start.7 = (bf16[1584,128]{1,0:T(8,128)(2,1)S(1)}, bf16[1584,128]{1,0:T(8,128)(2,1)S(1)}, u32[]{:S(2)}, u32[]{:S(2)}) collective-permute-start(bf16[1584,128]{1,0:T(8,128)(2,1)S(1)} %constant_dynamic-update-slice_fusion.4.refs_1_.refs_0_), channel_id=1, source_target_pairs={{0,8},{1,9},{2,10},{3,11},{4,12},{5,13},{6,14},{7,15},{8,16},{9,17... | collective-permute-start | bytes 1216520 | tf_op jit(solution)/shard_map/ppermute | solution.py:329
  32.2 20.8 %collective-permute-start.8 = (bf16[1584,128]{1,0:T(8,128)(2,1)S(1)}, bf16[1584,128]{1,0:T(8,128)(2,1)S(1)}, u32[]{:S(2)}, u32[]{:S(2)}) collective-permute-start(bf16[1584,128]{1,0:T(8,128)(2,1)S(1)} %constant_dynamic-update-slice_fusion.4.refs_1_.refs_0_), channel_id=1, source_target_pairs={{0,24},{1,25},{2,26},{3,27},{4,28},{5,29},{6,30},{7,31},{8,0},{9,1... | collective-permute-start | bytes 1216520 | tf_op jit(solution)/shard_map/ppermute | solution.py:329
  35.5 17.6 %collective-permute-start.9 = (bf16[1584,128]{1,0:T(8,128)(2,1)S(1)}, bf16[1584,128]{1,0:T(8,128)(2,1)S(1)}, u32[]{:S(2)}, u32[]{:S(2)}) collective-permute-start(bf16[1584,128]{1,0:T(8,128)(2,1)S(1)} %constant_dynamic-update-slice_fusion.4.refs_1_.refs_0_), channel_id=1, source_target_pairs={{0,16},{1,17},{2,18},{3,19},{4,20},{5,21},{6,22},{7,23},{8,24},{9,... | collective-permute-start | bytes 1216520 | tf_op jit(solution)/shard_map/ppermute | solution.py:329
  41.6 17.3 %collective-permute-start.10 = (bf16[2112,128]{1,0:T(8,128)(2,1)S(1)}, bf16[2112,128]{1,0:T(8,128)(2,1)S(1)}, u32[]{:S(2)}, u32[]{:S(2)}) collective-permute-start(bf16[2112,128]{1,0:T(8,128)(2,1)S(1)} %collective-permute-done.6.refs_0_.refs_1_), channel_id=1, source_target_pairs={{0,1},{1,2},{2,3},{3,4},{4,5},{5,6},{6,7},{7,0},{8,9},{9,10},{10,1... | collective-permute-start | bytes 1622024 | tf_op jit(solution)/shard_map/ppermute | solution.py:329
  42.7 16.2 %collective-permute-start.12 = (bf16[2112,128]{1,0:T(8,128)(2,1)S(1)}, bf16[2112,128]{1,0:T(8,128)(2,1)S(1)}, u32[]{:S(2)}, u32[]{:S(2)}) collective-permute-start(bf16[2112,128]{1,0:T(8,128)(2,1)S(1)} %collective-permute-done.11.refs_1_), channel_id=1, source_target_pairs={{0,7},{1,0},{2,1},{3,2},{4,3},{5,4},{6,5},{7,6},{8,15},{9,8},{10,9... | collective-permute-start | bytes 1622024 | tf_op jit(solution)/shard_map/ppermute | solution.py:329
  64.0 13.0 %collective-permute-start.14 = (bf16[272,1024]{1,0:T(8,128)(2,1)S(1)}, bf16[272,1024]{1,0:T(8,128)(2,1)S(1)}, u32[]{:S(2)}, u32[]{:S(2)}) collective-permute-start(bf16[272,1024]{1,0:T(8,128)(2,1)S(1)} %get-tuple-element.51), channel_id=1, source_target_pairs={{0,32},{1,33},{2,34},{3,35},{4,36},{5,37},{6,38},{7,39},{8,40},{9,... | collective-permute-start | bytes 1671176 | tf_op jit(solution)/shard_map/ppermute | solution.py:329
  64.3 12.7 %copy-start = (s32[256]{0:T(256)S(1)}, s32[256]{0:T(256)}, u32[]{:S(2)}) copy-start(s32[256]{0:T(256)} %pos_ref.5) | copy-start | bytes 3076
